TPU v7x, 32 devices: a whole 2x2x4 slice. The times are simulated.
32 devices in a mesh: section: 2 (over x), dp: 4 (over z), tensor: 4 (over y, core).
Axes of the slice: x: 2, y: 2, z: 4, core: 2. Of those that a mesh axis runs over, the one named last changes fastest.
Arguments:
- frames: bfloat16 [2, 1408, 768], P(None, ('dp', 'tensor')), may hold values from -6 to 6
- out_grad: bfloat16 [2, 1408, 768], P(None, ('dp', 'tensor')), may hold values from -6 to 6
- clip_ids: int32 [2, 1408], replicated, may hold values from 0 to 1, never falling along the last dimension, each value on 1 to 1232 neighbouring positions
- w_qkv: bfloat16 [2, 768, 3, 768], P('section', None, None, 'tensor'), may hold values from -0.21875 to 0.21875
- bias_qv: bfloat16 [2, 2, 768], P('section', None, 'tensor'), may hold values from -4 to 4
- w_out: bfloat16 [2, 768, 768], P('section', 'tensor'), may hold values from -2 to 2
- w_up: bfloat16 [2, 768, 3072], P('section', None, 'tensor'), may hold values from -0.21875 to 0.21875
- bias_up: bfloat16 [2, 3072], P('section', 'tensor'), may hold values from -4 to 4
- w_down: bfloat16 [2, 3072, 768], P('section', 'tensor'), may hold values from -0.109375 to 0.109375
- ln_gain: bfloat16 [2, 2, 768], P('section'), may hold values from 0.25 to 1.75
- shifts: bfloat16 [2, 4, 768], P('section'), may hold values from -4 to 4
Outputs:
- acts: bfloat16 [2, 2, 1408, 768], P('section', None, ('dp', 'tensor'))
- in_grads: bfloat16 [2, 2, 1408, 768], P('section', None, ('dp', 'tensor'))
- grad_qkv: float32 [2, 768, 3, 768], P('section', 'dp', None, 'tensor')
- grad_bias_qv: float32 [2, 2, 12, 64], P('section', None, 'tensor', 'dp')
- grad_out: float32 [2, 768, 768], P('section', 'tensor', 'dp')
- grad_up: float32 [2, 768, 3072], P('section', 'dp', 'tensor')
- grad_bias_up: float32 [2, 12, 256], P('section', 'tensor', 'dp')
- grad_down: float32 [2, 3072, 768], P('section', 'tensor', 'dp')
- grad_gain: float32 [2, 2, 768], P('section', None, ('dp', 'tensor'))
- grad_shift: float32 [2, 4, 768], P('section', None, ('dp', 'tensor'))
Inputs may be any that keep to these rules, and one draw needn't show every extreme that they name: `clip_ids`: clip numbers never fall along a micro-batch's frames; every clip has 1 to 1232 frames.
All inputs are finite; a program needn't handle non-finite values.
Results may differ from a plain program's by a relative error of at most 0.017.
Values may be sent and summed in bfloat16 or wider, within the bound.
A program may use at most 192 MiB of HBM per device.

v0:
```python
import jax
import jax.numpy as jnp
from jax import lax
from jax.sharding import PartitionSpec as P

HD = 64


def passed_along(block, axis, distance):
    devices = range(lax.axis_size(axis))
    route = [(i - distance, i) for i in devices if i - distance in devices]
    return lax.ppermute(block, axis, route)


def normalize(values, gain_row, shift_row):
    center = values - jnp.mean(values, axis=-1, keepdims=True)
    inverse = lax.rsqrt(jnp.mean(center * center, axis=-1, keepdims=True) + 1e-05)
    unit_rows = center * inverse
    return (unit_rows * gain_row + shift_row, unit_rows, inverse)


def norm_back(grad_rows, unit_rows, inverse, gain_row):
    scaled = grad_rows * gain_row
    result = inverse * (
        scaled
        - jnp.mean(scaled, axis=-1, keepdims=True)
        - unit_rows * jnp.mean(scaled * unit_rows, axis=-1, keepdims=True)
    )
    return (result, jnp.sum(grad_rows * unit_rows, axis=0), jnp.sum(grad_rows, axis=0))


def tensor_rows(local_rows):
    return lax.all_gather(local_rows, "tensor", axis=0, tiled=True)


def tensor_sum(left, right, form):
    return lax.psum_scatter(
        jnp.einsum(form, left, right, preferred_element_type=jnp.float32).astype(jnp.bfloat16),
        "tensor",
        scatter_dimension=0,
        tiled=True,
    ).astype(jnp.float32)


def masked_scores(query_part, key_part, same_clip):
    scores = (
        jnp.einsum("qhd,khd->qhk", query_part, key_part, preferred_element_type=jnp.float32) * 0.125
    )
    return jnp.where(same_clip[:, None, :], scores, -1e30)


def score_terms(query_part, grad_part, total_part, delta_part, key_part, value_part, same_clip):
    scores = masked_scores(query_part, key_part, same_clip)
    prob_rows = jnp.exp(scores - total_part[:, :, None])
    grad_prob = jnp.einsum(
        "qhd,khd->qhk", grad_part, value_part, preferred_element_type=jnp.float32
    )
    grad_score = (prob_rows * (grad_prob - delta_part[:, :, None])).astype(jnp.bfloat16)
    return (prob_rows.astype(jnp.bfloat16), grad_score)


def local(
    frames, out_grad, clip_ids, w_qkv, bias_qv, w_out, w_up, bias_up, w_down, ln_gain, shifts
):
    micro_count, own_rows, model_dim = frames.shape
    dp_rows = own_rows * lax.axis_size("tensor")
    slot_count = micro_count + 1
    section_idx = lax.axis_index("section")
    dp_idx = lax.axis_index("dp")
    qkv_weight = w_qkv[0]
    local_dim = qkv_weight.shape[2]
    head_count = local_dim // HD
    up_width = w_up.shape[2]
    query_bias = bias_qv[0, 0].astype(jnp.float32)
    value_bias = bias_qv[0, 1].astype(jnp.float32)
    out_weight = w_out[0]
    up_weight = w_up[0]
    up_bias = bias_up[0].astype(jnp.float32)
    down_weight = w_down[0]
    norm_gains = ln_gain[0].astype(jnp.float32)
    norm_shifts = shifts[0].astype(jnp.float32)

    def forward(layer_in, clip_all):
        layer_f = layer_in.astype(jnp.float32)
        normed_all = tensor_rows(
            normalize(layer_f, norm_gains[0], norm_shifts[0])[0].astype(jnp.bfloat16)
        )
        projected = jnp.einsum(
            "td,dcf->tcf", normed_all, qkv_weight, preferred_element_type=jnp.float32
        )
        queries = (
            (projected[:, 0] + query_bias).astype(jnp.bfloat16).reshape(dp_rows, head_count, HD)
        )
        key_rows = projected[:, 1].astype(jnp.bfloat16)
        value_rows = (projected[:, 2] + value_bias).astype(jnp.bfloat16)
        clip_row = lax.dynamic_slice_in_dim(clip_all, dp_idx * dp_rows, dp_rows, 0)
        key_part = lax.all_gather(key_rows, "dp", axis=0, tiled=True)
        run_peak = jnp.full((dp_rows, head_count), -1e30, jnp.float32)
        amount = key_part.shape[0]
        key_heads = key_part.reshape(amount, head_count, HD)
        same_clip = clip_row[:, None] == clip_all[None, :]
        scores = masked_scores(queries, key_heads, same_clip)
        new_peak = jnp.maximum(run_peak, jnp.max(scores, axis=-1))
        weights_e = jnp.where(same_clip[:, None, :], jnp.exp(scores - new_peak[:, :, None]), 0.0)
        run_total = jnp.sum(weights_e, axis=-1)
        run_peak, run_total = (new_peak, run_total)
        log_total = run_peak + jnp.log(run_total)
        key_part = lax.all_gather(key_rows, "dp", axis=0, tiled=True)
        value_part = lax.all_gather(value_rows, "dp", axis=0, tiled=True)
        amount = key_part.shape[0]
        key_heads = key_part.reshape(amount, head_count, HD)
        value_heads = value_part.reshape(amount, head_count, HD)
        same_clip = clip_row[:, None] == clip_all[None, :]
        scores = masked_scores(queries, key_heads, same_clip)
        prob_rows = jnp.where(same_clip[:, None, :], jnp.exp(scores - log_total[:, :, None]), 0.0)
        run_accum = jnp.einsum(
            "qhk,khd->qhd",
            prob_rows.astype(jnp.bfloat16),
            value_heads,
            preferred_element_type=jnp.float32,
        )
        run_exact = jnp.einsum(
            "qhk,khd->qhd",
            prob_rows,
            value_heads.astype(jnp.float32),
            precision=lax.Precision.HIGHEST,
        )
        run_accum, exact_attended = (run_accum, run_exact)
        attn_low = run_accum.astype(jnp.bfloat16).reshape(dp_rows, local_dim)
        hidden = layer_f + tensor_sum(attn_low, out_weight, "tf,fd->td") + norm_shifts[2]
        second_all = tensor_rows(
            normalize(hidden, norm_gains[1], norm_shifts[1])[0].astype(jnp.bfloat16)
        )
        up_proj = jnp.dot(second_all, up_weight, preferred_element_type=jnp.float32) + up_bias
        gelu_low = jax.nn.gelu(up_proj, approximate=False).astype(jnp.bfloat16)
        layer_out = hidden + tensor_sum(gelu_low, down_weight, "tf,fd->td") + norm_shifts[3]
        kept_vals = (
            normed_all,
            queries,
            key_rows.reshape(dp_rows, head_count, HD),
            value_rows.reshape(dp_rows, head_count, HD),
            exact_attended,
            log_total,
            hidden,
            second_all,
            up_proj,
            attn_low,
        )
        return (layer_out.astype(jnp.bfloat16), kept_vals)

    def backward(grad_in_low, kept_vals, layer_in, clip_all):
        (
            normed_all,
            queries,
            key_rows,
            value_rows,
            exact_attended,
            log_total,
            hidden,
            second_all,
            up_proj,
            attn_low,
        ) = kept_vals
        grad_f = grad_in_low.astype(jnp.float32)
        grad_all = tensor_rows(grad_in_low)
        gelu_vals, gelu_back = jax.vjp(lambda inner: jax.nn.gelu(inner, approximate=False), up_proj)
        gelu_low = gelu_vals.astype(jnp.bfloat16)
        grad_downw = jnp.einsum("tf,td->fd", gelu_low, grad_all, preferred_element_type=jnp.float32)
        grad_gelu = jnp.einsum(
            "td,fd->tf", grad_all, down_weight, preferred_element_type=jnp.float32
        )
        grad_up_in = gelu_back(grad_gelu)[0].astype(jnp.bfloat16)
        grad_upw = jnp.einsum(
            "td,tf->df", second_all, grad_up_in, preferred_element_type=jnp.float32
        )
        grad_upb = jnp.sum(grad_up_in.astype(jnp.float32), axis=0)
        grad_second = tensor_sum(grad_up_in, up_weight, "tf,df->td")
        unit_two, inverse_two = normalize(hidden, norm_gains[1], norm_shifts[1])[1:]
        back_two, grad_gain_two, grad_shift_two = norm_back(
            grad_second, unit_two, inverse_two, norm_gains[1]
        )
        grad_hidden = grad_f + back_two
        hidden_all = tensor_rows(grad_hidden.astype(jnp.bfloat16))
        grad_outw = jnp.einsum(
            "tf,td->fd", attn_low, hidden_all, preferred_element_type=jnp.float32
        )
        grad_attn = (
            jnp.einsum("td,fd->tf", hidden_all, out_weight, preferred_element_type=jnp.float32)
            .astype(jnp.bfloat16)
            .reshape(dp_rows, head_count, HD)
        )
        delta_rows = jnp.sum(grad_attn.astype(jnp.float32) * exact_attended, axis=-1)
        clip_row = lax.dynamic_slice_in_dim(clip_all, dp_idx * dp_rows, dp_rows, 0)
        key_flat = key_rows.reshape(dp_rows, local_dim)
        value_flat = value_rows.reshape(dp_rows, local_dim)
        key_part = lax.all_gather(key_flat, "dp", axis=0, tiled=True)
        value_part = lax.all_gather(value_flat, "dp", axis=0, tiled=True)
        amount = key_part.shape[0]
        key_heads = key_part.reshape(amount, head_count, HD)
        value_heads = value_part.reshape(amount, head_count, HD)
        same_clip = clip_row[:, None] == clip_all[None, :]
        prob_low, grad_score = score_terms(
            queries, grad_attn, log_total, delta_rows, key_heads, value_heads, same_clip
        )
        grad_query = jnp.einsum(
            "qhk,khd->qhd", grad_score, key_heads, preferred_element_type=jnp.float32
        )
        key_term = jnp.einsum(
            "qhk,qhd->khd", grad_score, queries, preferred_element_type=jnp.float32
        ).reshape(amount, local_dim)
        value_term = jnp.einsum(
            "qhk,qhd->khd", prob_low, grad_attn, preferred_element_type=jnp.float32
        ).reshape(amount, local_dim)
        folded = (grad_query, key_term, value_term)
        grad_query = folded[0]
        grad_key, grad_value = (
            lax.psum_scatter(
                folded[1].astype(jnp.bfloat16), "dp", scatter_dimension=0, tiled=True
            ).astype(jnp.float32),
            lax.psum_scatter(
                folded[2].astype(jnp.bfloat16), "dp", scatter_dimension=0, tiled=True
            ).astype(jnp.float32),
        )
        grad_key = grad_key.reshape(dp_rows, head_count, HD)
        grad_value = grad_value.reshape(dp_rows, head_count, HD)
        grad_low = (
            jnp.stack([grad_query * 0.125, grad_key * 0.125, grad_value], axis=1)
            .astype(jnp.bfloat16)
            .reshape(dp_rows, 3, local_dim)
        )
        grad_qkvw = jnp.einsum(
            "td,tcf->dcf", normed_all, grad_low, preferred_element_type=jnp.float32
        )
        column_sums = jnp.sum(grad_low.astype(jnp.float32), axis=0)
        grad_bias = jnp.stack([column_sums[0], column_sums[2]]).reshape(2, head_count, HD)
        grad_first = tensor_sum(grad_low, qkv_weight, "tcf,dcf->td")
        unit_one, inverse_one = normalize(
            layer_in.astype(jnp.float32), norm_gains[0], norm_shifts[0]
        )[1:]
        back_one, grad_gain_one, grad_shift_one = norm_back(
            grad_first, unit_one, inverse_one, norm_gains[0]
        )
        grad_input = (grad_hidden + back_one).astype(jnp.bfloat16)
        weight_terms = (
            grad_qkvw,
            grad_bias,
            grad_outw,
            grad_upw,
            grad_upb.reshape(head_count, up_width // head_count),
            grad_downw,
        )
        norm_terms = (
            jnp.stack([grad_gain_one, grad_gain_two]),
            jnp.stack(
                [
                    grad_shift_one,
                    grad_shift_two,
                    jnp.sum(grad_hidden, axis=0),
                    jnp.sum(grad_f, axis=0),
                ]
            ),
        )
        return (grad_input, weight_terms, norm_terms)

    kept_store = (
        jnp.zeros((slot_count, dp_rows, model_dim), jnp.bfloat16),
        jnp.zeros((slot_count, dp_rows, head_count, HD), jnp.bfloat16),
        jnp.zeros((slot_count, dp_rows, head_count, HD), jnp.bfloat16),
        jnp.zeros((slot_count, dp_rows, head_count, HD), jnp.bfloat16),
        jnp.zeros((slot_count, dp_rows, head_count, HD), jnp.float32),
        jnp.zeros((slot_count, dp_rows, head_count), jnp.float32),
        jnp.zeros((slot_count, own_rows, model_dim), jnp.float32),
        jnp.zeros((slot_count, dp_rows, model_dim), jnp.bfloat16),
        jnp.zeros((slot_count, dp_rows, up_width), jnp.float32),
        jnp.zeros((slot_count, dp_rows, local_dim), jnp.bfloat16),
    )
    row_zeros = jnp.zeros((slot_count, own_rows, model_dim), jnp.bfloat16)

    def fore_step(step_no, loop_state):
        received, kept_store, saved_in, act_store = loop_state
        own_idx = step_no - section_idx
        slot_idx = jnp.mod(own_idx, slot_count)
        micro_idx = jnp.clip(own_idx, 0, micro_count - 1)
        fresh_in = lax.dynamic_index_in_dim(
            frames, jnp.minimum(step_no, micro_count - 1), 0, keepdims=False
        )
        layer_in = jnp.where(section_idx == 0, fresh_in, received)
        clip_all = lax.dynamic_index_in_dim(clip_ids, micro_idx, 0, keepdims=False)
        layer_out, kept_vals = forward(layer_in, clip_all)
        kept_store = jax.tree.map(
            lambda buffer, new_leaf: lax.dynamic_update_index_in_dim(buffer, new_leaf, slot_idx, 0),
            kept_store,
            kept_vals,
        )
        saved_in = lax.dynamic_update_index_in_dim(saved_in, layer_in, slot_idx, 0)
        act_store = lax.dynamic_update_index_in_dim(act_store, layer_out, slot_idx, 0)
        received = passed_along(layer_out, "section", 1)
        return (received, kept_store, saved_in, act_store)

    fore_state = lax.fori_loop(
        0,
        slot_count,
        fore_step,
        (jnp.zeros((own_rows, model_dim), jnp.bfloat16), kept_store, row_zeros, row_zeros),
    )
    kept_store, saved_in, act_store = (fore_state[1], fore_state[2], fore_state[3])
    zero_weights = (
        jnp.zeros((model_dim, 3, local_dim), jnp.float32),
        jnp.zeros((2, head_count, HD), jnp.float32),
        jnp.zeros((local_dim, model_dim), jnp.float32),
        jnp.zeros((model_dim, up_width), jnp.float32),
        jnp.zeros((head_count, up_width // head_count), jnp.float32),
        jnp.zeros((up_width, model_dim), jnp.float32),
    )
    zero_norms = (jnp.zeros((2, model_dim), jnp.float32), jnp.zeros((4, model_dim), jnp.float32))

    def back_step(step_no, loop_state):
        received_grad, weight_sums, norm_sums, grad_store = loop_state
        own_idx = step_no - 1 + section_idx
        slot_idx = jnp.mod(own_idx, slot_count)
        micro_idx = jnp.clip(own_idx, 0, micro_count - 1)
        live_scale = ((own_idx >= 0) & (own_idx < micro_count)).astype(jnp.float32)
        given_grad = lax.dynamic_index_in_dim(out_grad, micro_idx, 0, keepdims=False)
        grad_in_low = jnp.where(section_idx == 1, given_grad, received_grad)
        kept_vals = jax.tree.map(
            lambda buffer: lax.dynamic_index_in_dim(buffer, slot_idx, 0, keepdims=False), kept_store
        )
        layer_in = lax.dynamic_index_in_dim(saved_in, slot_idx, 0, keepdims=False)
        clip_all = lax.dynamic_index_in_dim(clip_ids, micro_idx, 0, keepdims=False)
        grad_input, weight_terms, norm_terms = backward(grad_in_low, kept_vals, layer_in, clip_all)
        weight_sums = jax.tree.map(
            lambda total_sum, new_term: total_sum + live_scale * new_term, weight_sums, weight_terms
        )
        norm_sums = jax.tree.map(
            lambda total_sum, new_term: total_sum + live_scale * new_term, norm_sums, norm_terms
        )
        grad_store = lax.dynamic_update_index_in_dim(grad_store, grad_input, slot_idx, 0)
        received_grad = passed_along(grad_input, "section", -1)
        return (received_grad, weight_sums, norm_sums, grad_store)

    back_state = lax.fori_loop(
        0,
        slot_count,
        back_step,
        (jnp.zeros((own_rows, model_dim), jnp.bfloat16), zero_weights, zero_norms, row_zeros),
    )
    weight_sums, norm_sums, grad_store = (back_state[1], back_state[2], back_state[3])
    weight_parts = (
        lax.psum_scatter(
            weight_sums[0].astype(jnp.bfloat16), "dp", scatter_dimension=0, tiled=True
        ).astype(jnp.float32),
        lax.psum_scatter(
            weight_sums[1].astype(jnp.bfloat16), "dp", scatter_dimension=2, tiled=True
        ).astype(jnp.float32),
        lax.psum_scatter(
            weight_sums[2].astype(jnp.bfloat16), "dp", scatter_dimension=1, tiled=True
        ).astype(jnp.float32),
        lax.psum_scatter(
            weight_sums[3].astype(jnp.bfloat16), "dp", scatter_dimension=0, tiled=True
        ).astype(jnp.float32),
        lax.psum_scatter(
            weight_sums[4].astype(jnp.bfloat16), "dp", scatter_dimension=1, tiled=True
        ).astype(jnp.float32),
        lax.psum_scatter(
            weight_sums[5].astype(jnp.bfloat16), "dp", scatter_dimension=1, tiled=True
        ).astype(jnp.float32),
    )
    norm_parts = (
        lax.psum_scatter(norm_sums[0], ("dp", "tensor"), scatter_dimension=1, tiled=True),
        lax.psum_scatter(norm_sums[1], ("dp", "tensor"), scatter_dimension=1, tiled=True),
    )
    return (
        act_store[:micro_count][None],
        grad_store[:micro_count][None],
        weight_parts[0][None],
        weight_parts[1][None],
        weight_parts[2][None],
        weight_parts[3][None],
        weight_parts[4][None],
        weight_parts[5][None],
        norm_parts[0][None],
        norm_parts[1][None],
    )


def solution(mesh):
    in_specs = (
        P(None, ("dp", "tensor"), None),
        P(None, ("dp", "tensor"), None),
        P(),
        P("section", None, None, "tensor"),
        P("section", None, "tensor"),
        P("section", "tensor", None),
        P("section", None, "tensor"),
        P("section", "tensor"),
        P("section", "tensor", None),
        P("section", None, None),
        P("section", None, None),
    )
    out_specs = (
        P("section", None, ("dp", "tensor"), None),
        P("section", None, ("dp", "tensor"), None),
        P("section", "dp", None, "tensor"),
        P("section", None, "tensor", "dp"),
        P("section", "tensor", "dp"),
        P("section", "dp", "tensor"),
        P("section", "tensor", "dp"),
        P("section", "tensor", "dp"),
        P("section", None, ("dp", "tensor")),
        P("section", None, ("dp", "tensor")),
    )
    return jax.shard_map(local, mesh=mesh, in_specs=in_specs, out_specs=out_specs, check_vma=False)
```

profile of v0, /device:TPU:0, one launch (start us, length us, event | category | flops | bytes accessed | tf_op | source)
XLA Modules:
  0.0 1209.1 jit_solution(17249848476883856468)
XLA Ops:
  24.9 417.5 %while.75 = (s32[]{:T(128)}, bf16[88,768]{1,0:T(8,128)(2,1)}, bf16[3,352,768]{2,1,0:T(8,128)(2,1)}, bf16[3,352,3,64]{1,3,2,0:T(8,128)(2,1)}, bf16[3,352,3,64]{1,...) while((s32[]{:T(128)}, bf16[88,768]{1,0:T(8,128)(2,1)}, ...), condition=%wide.region_9.10_spmd, body=%wide.region_0.9_spmd.sunk | while | flops 2807192832 | bytes 103197208 | solution.py:300
  29.9 8.7 all_gather.95
  41.7 17.5 %all-gather.10 = bf16[4,352,192]{1,2,0:T(8,128)(2,1)S(1)} all-gather(bf16[1,352,192]{1,2,0:T(8,128)(2,1)S(1)} %fusion.294), channel_id=1, replica_groups=mesh['section'=2,'dp'=4,'tensor'=4] {'dp'}, dimensions={0}, use_global_device_ids=true | all-gather | bytes 675840 | tf_op jit(solution)/shard_map/while/body/eval_jaxpr/all_gather | solution.py:109
  60.9 26.5 %all-gather.11 = bf16[1408,1,192]{2,1,0:T(2,128)(2,1)S(1)} all-gather(bf16[352,1,192]{2,1,0:T(2,128)(2,1)S(1)} %copy.93), channel_id=2, replica_groups=mesh['section'=2,'dp'=4,'tensor'=4] {'dp'}, dimensions={0}, use_global_device_ids=true | all-gather | bytes 675840 | tf_op jit(solution)/shard_map/while/body/eval_jaxpr/all_gather | solution.py:108
  99.7 19.6 %reduce-scatter.51.cloned.1.call-done = bf16[88,768]{1,0:T(8,128)(2,1)} async-done(((bf16[352,768]{1,0:T(8,128)(2,1)}), bf16[88,768]{1,0:T(8,128)(2,1)}) %reduce-scatter.51.cloned.1.call-update) | async-done | bytes 135184 | tf_op jit(solution)/shard_map/while/body/eval_jaxpr/reduce_scatter | solution.py:37
  122.5 6.9 all_gather.96
  136.2 7.5 fusion.300
  144.6 12.4 %reduce-scatter.53.cloned.1.call-done = bf16[88,768]{1,0:T(8,128)(2,1)} async-done(((bf16[352,768]{1,0:T(8,128)(2,1)}), bf16[88,768]{1,0:T(8,128)(2,1)}) %reduce-scatter.53.cloned.1.call-update) | async-done | bytes 135184 | tf_op jit(solution)/shard_map/while/body/eval_jaxpr/reduce_scatter | solution.py:37
  169.9 6.6 all_gather.95
  179.6 17.2 %all-gather.10 = bf16[4,352,192]{1,2,0:T(8,128)(2,1)S(1)} all-gather(bf16[1,352,192]{1,2,0:T(8,128)(2,1)S(1)} %fusion.294), channel_id=1, replica_groups=mesh['section'=2,'dp'=4,'tensor'=4] {'dp'}, dimensions={0}, use_global_device_ids=true | all-gather | bytes 675840 | tf_op jit(solution)/shard_map/while/body/eval_jaxpr/all_gather | solution.py:109
  198.4 26.4 %all-gather.11 = bf16[1408,1,192]{2,1,0:T(2,128)(2,1)S(1)} all-gather(bf16[352,1,192]{2,1,0:T(2,128)(2,1)S(1)} %copy.93), channel_id=2, replica_groups=mesh['section'=2,'dp'=4,'tensor'=4] {'dp'}, dimensions={0}, use_global_device_ids=true | all-gather | bytes 675840 | tf_op jit(solution)/shard_map/while/body/eval_jaxpr/all_gather | solution.py:108
  237.3 20.8 %reduce-scatter.51.cloned.1.call-done = bf16[88,768]{1,0:T(8,128)(2,1)} async-done(((bf16[352,768]{1,0:T(8,128)(2,1)}), bf16[88,768]{1,0:T(8,128)(2,1)}) %reduce-scatter.51.cloned.1.call-update) | async-done | bytes 135184 | tf_op jit(solution)/shard_map/while/body/eval_jaxpr/reduce_scatter | solution.py:37
  261.3 6.9 all_gather.96
  275.0 7.5 fusion.300
  283.4 12.4 %reduce-scatter.53.cloned.1.call-done = bf16[88,768]{1,0:T(8,128)(2,1)} async-done(((bf16[352,768]{1,0:T(8,128)(2,1)}), bf16[88,768]{1,0:T(8,128)(2,1)}) %reduce-scatter.53.cloned.1.call-update) | async-done | bytes 135184 | tf_op jit(solution)/shard_map/while/body/eval_jaxpr/reduce_scatter | solution.py:37
  308.7 6.6 all_gather.95
  318.3 17.2 %all-gather.10 = bf16[4,352,192]{1,2,0:T(8,128)(2,1)S(1)} all-gather(bf16[1,352,192]{1,2,0:T(8,128)(2,1)S(1)} %fusion.294), channel_id=1, replica_groups=mesh['section'=2,'dp'=4,'tensor'=4] {'dp'}, dimensions={0}, use_global_device_ids=true | all-gather | bytes 675840 | tf_op jit(solution)/shard_map/while/body/eval_jaxpr/all_gather | solution.py:109
  337.2 26.5 %all-gather.11 = bf16[1408,1,192]{2,1,0:T(2,128)(2,1)S(1)} all-gather(bf16[352,1,192]{2,1,0:T(2,128)(2,1)S(1)} %copy.93), channel_id=2, replica_groups=mesh['section'=2,'dp'=4,'tensor'=4] {'dp'}, dimensions={0}, use_global_device_ids=true | all-gather | bytes 675840 | tf_op jit(solution)/shard_map/while/body/eval_jaxpr/all_gather | solution.py:108
  376.1 20.8 %reduce-scatter.51.cloned.1.call-done = bf16[88,768]{1,0:T(8,128)(2,1)} async-done(((bf16[352,768]{1,0:T(8,128)(2,1)}), bf16[88,768]{1,0:T(8,128)(2,1)}) %reduce-scatter.51.cloned.1.call-update) | async-done | bytes 135184 | tf_op jit(solution)/shard_map/while/body/eval_jaxpr/reduce_scatter | solution.py:37
  400.2 6.8 all_gather.96
  413.8 7.5 fusion.300
  422.3 12.3 %reduce-scatter.53.cloned.1.call-done = bf16[88,768]{1,0:T(8,128)(2,1)} async-done(((bf16[352,768]{1,0:T(8,128)(2,1)}), bf16[88,768]{1,0:T(8,128)(2,1)}) %reduce-scatter.53.cloned.1.call-update) | async-done | bytes 135184 | tf_op jit(solution)/shard_map/while/body/eval_jaxpr/reduce_scatter | solution.py:37
  443.3 490.0 %while.76 = (s32[]{:T(128)}, bf16[88,768]{1,0:T(8,128)(2,1)S(1)}, f32[768,3,192]{0,2,1:T(8,128)}, f32[2,3,64]{2,1,0:T(4,128)}, f32[192,768]{1,0:T(8,128)}, /*ind...) while((s32[]{:T(128)}, bf16[88,768]{1,0:T(8,128)(2,1)S(1)}, ...), condition=%wide.region_32.33_spmd.clone, body=%wide.region_10.32_spmd.clone.sunk | while | flops 3486401536 | bytes 139980880 | solution.py:341
  444.4 6.6 all_gather.97
  464.5 17.2 %all-gather.12 = bf16[4,352,192]{1,2,0:T(8,128)(2,1)S(1)} all-gather(bf16[1,352,192]{1,2,0:T(8,128)(2,1)S(1)} %bitcast.481), channel_id=1, replica_groups=mesh['section'=2,'dp'=4,'tensor'=4] {'dp'}, dimensions={0}, use_global_device_ids=true | all-gather | bytes 675840 | tf_op jit(solution)/shard_map/while/body/eval_jaxpr/all_gather | solution.py:196
  482.6 16.1 %all-gather.13 = bf16[4,352,192]{1,2,0:T(8,128)(2,1)S(1)} all-gather(bf16[1,352,192]{1,2,0:T(8,128)(2,1)S(1)} %bitcast.480), channel_id=1, replica_groups=mesh['section'=2,'dp'=4,'tensor'=4] {'dp'}, dimensions={0}, use_global_device_ids=true | all-gather | bytes 675840 | tf_op jit(solution)/shard_map/while/body/eval_jaxpr/all_gather | solution.py:197
  508.9 7.1 all_gather.98
  542.7 7.0 reduce-scatter.59.cloned.1.call-done
  550.8 23.2 %reduce-scatter.57.cloned.1.call-done = bf16[352,192]{1,0:T(8,128)(2,1)} async-done(((bf16[1408,192]{1,0:T(8,128)(2,1)}), bf16[352,192]{1,0:T(8,128)(2,1)}) %reduce-scatter.57.cloned.1.call-update) | async-done | bytes 135184 | tf_op jit(solution)/shard_map/while
  579.3 18.4 %reduce-scatter.61.cloned.1.call-done = bf16[88,768]{1,0:T(8,128)(2,1)} async-done(((bf16[352,768]{1,0:T(8,128)(2,1)}), bf16[88,768]{1,0:T(8,128)(2,1)}) %reduce-scatter.61.cloned.1.call-update) | async-done | bytes 135184 | tf_op jit(solution)/shard_map/while/body/eval_jaxpr/reduce_scatter | solution.py:37
  609.2 6.6 all_gather.97
  629.4 17.2 %all-gather.12 = bf16[4,352,192]{1,2,0:T(8,128)(2,1)S(1)} all-gather(bf16[1,352,192]{1,2,0:T(8,128)(2,1)S(1)} %bitcast.481), channel_id=1, replica_groups=mesh['section'=2,'dp'=4,'tensor'=4] {'dp'}, dimensions={0}, use_global_device_ids=true | all-gather | bytes 675840 | tf_op jit(solution)/shard_map/while/body/eval_jaxpr/all_gather | solution.py:196
  647.5 16.1 %all-gather.13 = bf16[4,352,192]{1,2,0:T(8,128)(2,1)S(1)} all-gather(bf16[1,352,192]{1,2,0:T(8,128)(2,1)S(1)} %bitcast.480), channel_id=1, replica_groups=mesh['section'=2,'dp'=4,'tensor'=4] {'dp'}, dimensions={0}, use_global_device_ids=true | all-gather | bytes 675840 | tf_op jit(solution)/shard_map/while/body/eval_jaxpr/all_gather | solution.py:197
  673.8 7.2 all_gather.98
  713.6 23.0 %reduce-scatter.57.cloned.1.call-done = bf16[352,192]{1,0:T(8,128)(2,1)} async-done(((bf16[1408,192]{1,0:T(8,128)(2,1)}), bf16[352,192]{1,0:T(8,128)(2,1)}) %reduce-scatter.57.cloned.1.call-update) | async-done | bytes 135184 | tf_op jit(solution)/shard_map/while
  742.0 18.3 %reduce-scatter.61.cloned.1.call-done = bf16[88,768]{1,0:T(8,128)(2,1)} async-done(((bf16[352,768]{1,0:T(8,128)(2,1)}), bf16[88,768]{1,0:T(8,128)(2,1)}) %reduce-scatter.61.cloned.1.call-update) | async-done | bytes 135184 | tf_op jit(solution)/shard_map/while/body/eval_jaxpr/reduce_scatter | solution.py:37
  792.0 17.2 %all-gather.12 = bf16[4,352,192]{1,2,0:T(8,128)(2,1)S(1)} all-gather(bf16[1,352,192]{1,2,0:T(8,128)(2,1)S(1)} %bitcast.481), channel_id=1, replica_groups=mesh['section'=2,'dp'=4,'tensor'=4] {'dp'}, dimensions={0}, use_global_device_ids=true | all-gather | bytes 675840 | tf_op jit(solution)/shard_map/while/body/eval_jaxpr/all_gather | solution.py:196
  810.1 16.1 %all-gather.13 = bf16[4,352,192]{1,2,0:T(8,128)(2,1)S(1)} all-gather(bf16[1,352,192]{1,2,0:T(8,128)(2,1)S(1)} %bitcast.480), channel_id=1, replica_groups=mesh['section'=2,'dp'=4,'tensor'=4] {'dp'}, dimensions={0}, use_global_device_ids=true | all-gather | bytes 675840 | tf_op jit(solution)/shard_map/while/body/eval_jaxpr/all_gather | solution.py:197
  836.4 7.2 all_gather.98
  876.3 22.8 %reduce-scatter.57.cloned.1.call-done = bf16[352,192]{1,0:T(8,128)(2,1)} async-done(((bf16[1408,192]{1,0:T(8,128)(2,1)}), bf16[352,192]{1,0:T(8,128)(2,1)}) %reduce-scatter.57.cloned.1.call-update) | async-done | bytes 135184 | tf_op jit(solution)/shard_map/while
  904.5 18.3 %reduce-scatter.61.cloned.1.call-done = bf16[88,768]{1,0:T(8,128)(2,1)} async-done(((bf16[352,768]{1,0:T(8,128)(2,1)}), bf16[88,768]{1,0:T(8,128)(2,1)}) %reduce-scatter.61.cloned.1.call-update) | async-done | bytes 135184 | tf_op jit(solution)/shard_map/while/body/eval_jaxpr/reduce_scatter | solution.py:37
  955.4 18.5 %reduce-scatter.45.cloned.1.call-done = bf16[64,3]{1,0:T(8,128)(2,1)} async-done(((bf16[256,3]{1,0:T(8,128)(2,1)}), bf16[64,3]{1,0:T(8,128)(2,1)}) %reduce-scatter.45.cloned.1.call-update) | async-done | bytes 400
  975.3 56.3 %reduce-scatter.47.cloned.1.call-done = f32[48,2]{1,0:T(8,128)} async-done(((f32[768,2]{1,0:T(8,128)}), f32[48,2]{1,0:T(8,128)}) %reduce-scatter.47.cloned.1.call-update) | async-done | bytes 400
  1033.0 57.7 %reduce-scatter.49.cloned.1.call-done = f32[48,4]{1,0:T(8,128)} async-done(((f32[768,4]{1,0:T(8,128)}), f32[48,4]{1,0:T(8,128)}) %reduce-scatter.49.cloned.1.call-update) | async-done | bytes 784
  1092.1 21.2 %reduce-scatter.43.cloned.1.call-done = bf16[192,192]{1,0:T(8,128)(2,1)} async-done(((bf16[768,192]{1,0:T(8,128)(2,1)}), bf16[192,192]{1,0:T(8,128)(2,1)}) %reduce-scatter.43.cloned.1.call-update) | async-done | bytes 73744
  1115.0 25.0 %reduce-scatter.39.cloned.1.call-done = bf16[192,576]{1,0:T(8,128)(2,1)} async-done(((bf16[768,576]{1,0:T(8,128)(2,1)}), bf16[192,576]{1,0:T(8,128)(2,1)}) %reduce-scatter.39.cloned.1.call-update) | async-done | bytes 221200
  1142.1 27.8 %reduce-scatter.35.cloned.1.call-done = bf16[192,768]{1,0:T(8,128)(2,1)} async-done(((bf16[768,768]{1,0:T(8,128)(2,1)}), bf16[192,768]{1,0:T(8,128)(2,1)}) %reduce-scatter.35.cloned.1.call-update) | async-done | bytes 294928 | tf_op jit(solution)/shard_map/reduce_scatter | solution.py:358
  1171.7 28.2 %reduce-scatter.37.cloned.1.call-done = bf16[768,192]{0,1:T(8,128)(2,1)} async-done(((bf16[768,768]{0,1:T(8,128)(2,1)}), bf16[768,192]{0,1:T(8,128)(2,1)}) %reduce-scatter.37.cloned.1.call-update) | async-done | bytes 294928 | tf_op jit(solution)/shard_map/reduce_scatter | solution.py:364
  (777 shorter events, 395.3 us)
Async XLA Ops:
  24.9 94.4 %reduce-scatter.51.cloned.1.call-start = ((), (), s32[]{:S(2)}) async-start(), calls=%async_computation.22 | async-start | bytes 675840 | tf_op jit(solution)/shard_map/while/body/eval_jaxpr/reduce_scatter | solution.py:37
  40.2 50.0 %copy-start.34 = (f32[3,64]{1,0:T(4,128)}, f32[3,64]{1,0:T(4,128)S(1)}, u32[]{:S(2)}) copy-start(f32[3,64]{1,0:T(4,128)S(1)} %add.910) | copy-start | bytes 2308 | tf_op jit(solution)/shard_map/while
  97.4 59.7 %reduce-scatter.53.cloned.1.call-start = ((), (), s32[]{:S(2)}) async-start(), calls=%async_computation.23 | async-start | bytes 675840 | tf_op jit(solution)/shard_map/while/body/eval_jaxpr/reduce_scatter | solution.py:37
  98.9 30.6 %copy-start.18 = (bf16[768,768]{1,0:T(8,128)(2,1)S(1)}, bf16[768,768]{1,0:T(8,128)(2,1)}, u32[]{:S(2)}) copy-start(bf16[768,768]{1,0:T(8,128)(2,1)} %get-tuple-element.2566) | copy-start | bytes 3538948 | tf_op jit(solution)/shard_map/while
  98.9 30.6 %copy-start.45 = (f32[768]{0:T(1024)S(1)}, f32[768]{0:T(1024)}, u32[]{:S(2)}) copy-start(f32[768]{0:T(1024)} %get-tuple-element.2567) | copy-start | bytes 9220 | tf_op jit(solution)/shard_map/while
  158.7 6.2 collective-permute-start
  164.9 93.2 %reduce-scatter.51.cloned.1.call-start = ((), (), s32[]{:S(2)}) async-start(), calls=%async_computation.22 | async-start | bytes 675840 | tf_op jit(solution)/shard_map/while/body/eval_jaxpr/reduce_scatter | solution.py:37
  178.0 49.7 %copy-start.34 = (f32[3,64]{1,0:T(4,128)}, f32[3,64]{1,0:T(4,128)S(1)}, u32[]{:S(2)}) copy-start(f32[3,64]{1,0:T(4,128)S(1)} %add.910) | copy-start | bytes 2308 | tf_op jit(solution)/shard_map/while
  234.9 60.9 %reduce-scatter.53.cloned.1.call-start = ((), (), s32[]{:S(2)}) async-start(), calls=%async_computation.23 | async-start | bytes 675840 | tf_op jit(solution)/shard_map/while/body/eval_jaxpr/reduce_scatter | solution.py:37
  236.4 31.8 %copy-start.18 = (bf16[768,768]{1,0:T(8,128)(2,1)S(1)}, bf16[768,768]{1,0:T(8,128)(2,1)}, u32[]{:S(2)}) copy-start(bf16[768,768]{1,0:T(8,128)(2,1)} %get-tuple-element.2566) | copy-start | bytes 3538948 | tf_op jit(solution)/shard_map/while
  236.4 31.8 %copy-start.45 = (f32[768]{0:T(1024)S(1)}, f32[768]{0:T(1024)}, u32[]{:S(2)}) copy-start(f32[768]{0:T(1024)} %get-tuple-element.2567) | copy-start | bytes 9220 | tf_op jit(solution)/shard_map/while
  297.5 6.2 collective-permute-start
  303.7 93.2 %reduce-scatter.51.cloned.1.call-start = ((), (), s32[]{:S(2)}) async-start(), calls=%async_computation.22 | async-start | bytes 675840 | tf_op jit(solution)/shard_map/while/body/eval_jaxpr/reduce_scatter | solution.py:37
  316.8 49.7 %copy-start.34 = (f32[3,64]{1,0:T(4,128)}, f32[3,64]{1,0:T(4,128)S(1)}, u32[]{:S(2)}) copy-start(f32[3,64]{1,0:T(4,128)S(1)} %add.910) | copy-start | bytes 2308 | tf_op jit(solution)/shard_map/while
  373.7 60.8 %reduce-scatter.53.cloned.1.call-start = ((), (), s32[]{:S(2)}) async-start(), calls=%async_computation.23 | async-start | bytes 675840 | tf_op jit(solution)/shard_map/while/body/eval_jaxpr/reduce_scatter | solution.py:37
  375.2 31.8 %copy-start.18 = (bf16[768,768]{1,0:T(8,128)(2,1)S(1)}, bf16[768,768]{1,0:T(8,128)(2,1)}, u32[]{:S(2)}) copy-start(bf16[768,768]{1,0:T(8,128)(2,1)} %get-tuple-element.2566) | copy-start | bytes 3538948 | tf_op jit(solution)/shard_map/while
  375.2 31.8 %copy-start.45 = (f32[768]{0:T(1024)S(1)}, f32[768]{0:T(1024)}, u32[]{:S(2)}) copy-start(f32[768]{0:T(1024)} %get-tuple-element.2567) | copy-start | bytes 9220 | tf_op jit(solution)/shard_map/while
  436.2 6.2 collective-permute-start
  443.3 63.3 %reduce-scatter.55.cloned.1.call-start = ((), (), s32[]{:S(2)}) async-start(), calls=%async_computation.24 | async-start | bytes 675840 | tf_op jit(solution)/shard_map/while/body/eval_jaxpr/reduce_scatter | solution.py:37
  458.0 91.7 %reduce-scatter.59.cloned.1.call-start = ((), (), s32[]{:S(2)}) async-start(), calls=%async_computation.26 | async-start | bytes 901120 | tf_op jit(solution)/shard_map/while
  525.7 48.2 %reduce-scatter.57.cloned.1.call-start = ((), (), s32[]{:S(2)}) async-start(), calls=%async_computation.25 | async-start | bytes 901120 | tf_op jit(solution)/shard_map/while
  539.4 58.2 %reduce-scatter.61.cloned.1.call-start = ((), (), s32[]{:S(2)}) async-start(), calls=%async_computation.27 | async-start | bytes 675840 | tf_op jit(solution)/shard_map/while/body/eval_jaxpr/reduce_scatter | solution.py:37
  542.7 32.5 %copy-start.27 = (bf16[768,3,192]{0,2,1:T(8,128)(2,1)S(1)}, bf16[768,3,192]{0,2,1:T(8,128)(2,1)}, u32[]{:S(2)}) copy-start(bf16[768,3,192]{0,2,1:T(8,128)(2,1)} %copy-done.26) | copy-start | bytes 2654212 | tf_op jit(solution)/shard_map/while
  579.2 28.7 %copy-start.4 = (f32[768,3,192]{0,2,1:T(8,128)}, f32[768,3,192]{0,2,1:T(8,128)S(1)}, u32[]{:S(2)}) copy-start(f32[768,3,192]{0,2,1:T(8,128)S(1)} %select_add_fusion.10) | copy-start | bytes 5308420 | tf_op jit(solution)/shard_map/while
  579.3 28.7 %copy-start.53 = (f32[3,352,3]{1,2,0:T(4,128)S(1)}, f32[3,352,3]{1,2,0:T(4,128)}, u32[]{:S(2)}) copy-start(f32[3,352,3]{1,2,0:T(4,128)} %copy-done.52) | copy-start | bytes 38020 | tf_op jit(solution)/shard_map/while
  600.7 7.2 collective-permute-start.1
  608.0 63.5 %reduce-scatter.55.cloned.1.call-start = ((), (), s32[]{:S(2)}) async-start(), calls=%async_computation.24 | async-start | bytes 675840 | tf_op jit(solution)/shard_map/while/body/eval_jaxpr/reduce_scatter | solution.py:37
  622.9 89.7 %reduce-scatter.59.cloned.1.call-start = ((), (), s32[]{:S(2)}) async-start(), calls=%async_computation.26 | async-start | bytes 901120 | tf_op jit(solution)/shard_map/while
  690.6 46.0 %reduce-scatter.57.cloned.1.call-start = ((), (), s32[]{:S(2)}) async-start(), calls=%async_computation.25 | async-start | bytes 901120 | tf_op jit(solution)/shard_map/while
  705.9 54.4 %reduce-scatter.61.cloned.1.call-start = ((), (), s32[]{:S(2)}) async-start(), calls=%async_computation.27 | async-start | bytes 675840 | tf_op jit(solution)/shard_map/while/body/eval_jaxpr/reduce_scatter | solution.py:37
  741.9 28.7 %copy-start.4 = (f32[768,3,192]{0,2,1:T(8,128)}, f32[768,3,192]{0,2,1:T(8,128)S(1)}, u32[]{:S(2)}) copy-start(f32[768,3,192]{0,2,1:T(8,128)S(1)} %select_add_fusion.10) | copy-start | bytes 5308420 | tf_op jit(solution)/shard_map/while
  741.9 28.6 %copy-start.53 = (f32[3,352,3]{1,2,0:T(4,128)S(1)}, f32[3,352,3]{1,2,0:T(4,128)}, u32[]{:S(2)}) copy-start(f32[3,352,3]{1,2,0:T(4,128)} %copy-done.52) | copy-start | bytes 38020 | tf_op jit(solution)/shard_map/while
  763.4 7.2 collective-permute-start.1
  770.6 63.4 %reduce-scatter.55.cloned.1.call-start = ((), (), s32[]{:S(2)}) async-start(), calls=%async_computation.24 | async-start | bytes 675840 | tf_op jit(solution)/shard_map/while/body/eval_jaxpr/reduce_scatter | solution.py:37
  785.5 89.7 %reduce-scatter.59.cloned.1.call-start = ((), (), s32[]{:S(2)}) async-start(), calls=%async_computation.26 | async-start | bytes 901120 | tf_op jit(solution)/shard_map/while
  853.3 45.9 %reduce-scatter.57.cloned.1.call-start = ((), (), s32[]{:S(2)}) async-start(), calls=%async_computation.25 | async-start | bytes 901120 | tf_op jit(solution)/shard_map/while
  868.5 54.3 %reduce-scatter.61.cloned.1.call-start = ((), (), s32[]{:S(2)}) async-start(), calls=%async_computation.27 | async-start | bytes 675840 | tf_op jit(solution)/shard_map/while/body/eval_jaxpr/reduce_scatter | solution.py:37
  904.4 28.6 %copy-start.4 = (f32[768,3,192]{0,2,1:T(8,128)}, f32[768,3,192]{0,2,1:T(8,128)S(1)}, u32[]{:S(2)}) copy-start(f32[768,3,192]{0,2,1:T(8,128)S(1)} %select_add_fusion.10) | copy-start | bytes 5308420 | tf_op jit(solution)/shard_map/while
  904.4 28.6 %copy-start.53 = (f32[3,352,3]{1,2,0:T(4,128)S(1)}, f32[3,352,3]{1,2,0:T(4,128)}, u32[]{:S(2)}) copy-start(f32[3,352,3]{1,2,0:T(4,128)} %copy-done.52) | copy-start | bytes 38020 | tf_op jit(solution)/shard_map/while
  925.9 7.2 collective-permute-start.1
  933.3 20.7 %reduce-scatter.41.cloned.1.call-start = ((), (), s32[]{:S(2)}) async-start(), calls=%async_computation.17 | async-start | bytes 20480
  934.9 39.0 %reduce-scatter.45.cloned.1.call-start = ((), (), s32[]{:S(2)}) async-start(), calls=%async_computation.19 | async-start | bytes 81920
  936.5 95.2 %reduce-scatter.47.cloned.1.call-start = ((), (), s32[]{:S(2)}) async-start(), calls=%async_computation.20 | async-start | bytes 417792
  938.2 152.6 %reduce-scatter.49.cloned.1.call-start = ((), (), s32[]{:S(2)}) async-start(), calls=%async_computation.21 | async-start | bytes 417792
  939.9 173.4 %reduce-scatter.43.cloned.1.call-start = ((), (), s32[]{:S(2)}) async-start(), calls=%async_computation.18 | async-start | bytes 491520
  940.9 199.1 %reduce-scatter.39.cloned.1.call-start = ((), (), s32[]{:S(2)}) async-start(), calls=%async_computation.16 | async-start | bytes 1228800
  943.0 226.9 %reduce-scatter.35.cloned.1.call-start = ((), (), s32[]{:S(2)}) async-start(), calls=%async_computation.14 | async-start | bytes 1474560 | tf_op jit(solution)/shard_map/reduce_scatter | solution.py:358
  944.8 255.1 %reduce-scatter.37.cloned.1.call-start = ((), (), s32[]{:S(2)}) async-start(), calls=%async_computation.15 | async-start | bytes 1474560 | tf_op jit(solution)/shard_map/reduce_scatter | solution.py:364
  (152 other events, 1369.2 us)
Sparse Core Ops, SparseCore 0:
  97.5 21.7 reduce-scatter.50
  134.8 22.1 reduce-scatter.52
  235.1 22.9 reduce-scatter.50
  273.6 22.1 reduce-scatter.52
  373.9 23.0 reduce-scatter.50
  412.4 22.0 reduce-scatter.52
  458.1 23.5 reduce-scatter.54
  525.9 23.7 reduce-scatter.58
  552.0 21.9 reduce-scatter.56
  576.9 20.7 reduce-scatter.60
  623.0 21.5 reduce-scatter.54
  690.8 21.7 reduce-scatter.58
  714.8 21.7 reduce-scatter.56
  739.6 20.6 reduce-scatter.60
  785.6 21.5 reduce-scatter.54
  853.4 21.7 reduce-scatter.58
  877.3 21.7 reduce-scatter.56
  902.0 20.6 reduce-scatter.60
Sparse Core Ops, SparseCore 1:
  936.0 17.9 reduce-scatter.40
  956.8 17.1 reduce-scatter.44
  977.9 53.7 reduce-scatter.46
  1036.2 54.5 reduce-scatter.48
  1093.6 19.6 reduce-scatter.42
  1115.8 24.2 reduce-scatter.38
  1142.2 27.6 reduce-scatter.34
  1172.1 27.8 reduce-scatter.36
where the time goes:
time: 1210 us
  waiting for transfers between devices  497 us (41%)
  blocking collectives  315 us (26%)
  matrix products  164 us (14%)
  local copies, waits for them, and re-layouts  119 us (10%)
  other arithmetic  78.4 us (6%)
  starting transfers between devices  17 us (1%)
  between operations  15.8 us (1%)
    unnamed x14, waiting for transfers between devices  183 us
    reduce_scatter x12, waiting for transfers between devices, tensor_sum(): lax.psum_scatter(jnp.einsum(form, left, right, preferred_element_type=jnp...  153 us
    all_gather x12, blocking collectives, tensor_rows(): return lax.all_gather(local_rows, 'tensor', axis=0, tiled=True)  83.6 us
    while x24, waiting for transfers between devices  82.5 us
    all_gather x3, blocking collectives, forward(): key_part = lax.all_gather(key_rows, 'dp', axis=0, tiled=True)  79.4 us
    all_gather x3, blocking collectives, forward(): value_part = lax.all_gather(value_rows, 'dp', axis=0, tiled=True)  51.9 us
    all_gather x3, blocking collectives, backward(): key_part = lax.all_gather(key_flat, 'dp', axis=0, tiled=True)  51.6 us
    all_gather x3, blocking collectives, backward(): value_part = lax.all_gather(value_flat, 'dp', axis=0, tiled=True)  48.3 us
  transfers between devices with their start and end apart: 32, of which 29 were waited for; matrix products, arithmetic and copies ran while one was open for 14% of the time, Pallas kernels for 0%

commit v1 on v0

v1 whole, which is shorter than its diff:
```python
import functools

import jax
import jax.numpy as jnp
from jax import lax
from jax.experimental import pallas as pl
from jax.experimental.pallas import tpu as pltpu
from jax.sharding import PartitionSpec as P

HD = 64
BIG = 2.0**100
MESH = pl.DeviceIdType.MESH
BF = jnp.bfloat16
F32 = jnp.float32
RB = 16
SLOTS = 4
MOST = 4


def nt(a, b):
    return lax.dot_general(a, b, (((1,), (1,)), ((), ())), preferred_element_type=F32)


def nn(a, b):
    return lax.dot_general(a, b, (((1,), (0,)), ((), ())), preferred_element_type=F32)


def tn(a, b):
    return lax.dot_general(a, b, (((0,), (0,)), ((), ())), preferred_element_type=F32)


def scratch_plan(nd, rows, dim, head_dim, ff):
    half = nd // 2
    full = 4 * rows
    two = 2 * rows
    part = dim // nd
    wide = 640 + ff + 256 + ff
    vm = pltpu.VMEM
    dma = pltpu.SemaphoreType.DMA
    return dict(
        wqb=vm((2, 640, dim), BF),
        wob=vm((2, 256, dim), BF),
        wub=vm((2, dim, ff), BF),
        wdb=vm((2, ff, dim), BF),
        spb=vm((2, 16, dim), F32),
        xq=vm((2, rows, dim), BF),
        gq=vm((2, rows, dim), BF),
        xres=vm((two, dim), F32),
        dyf=vm((two, dim), F32),
        dyb=vm((2, 2, two, dim), BF),
        nb=vm((2, 2, two, dim), BF),
        sb=vm((2, 2, two, dim), BF),
        hid=vm((two, dim), F32),
        u1=vm((2, two, dim), F32),
        u2=vm((2, two, dim), F32),
        r1=vm((2, two, 1), F32),
        r2=vm((2, two, 1), F32),
        qa=vm((2, full, 256), BF),
        kvb=vm((2, nd, full, 384), BF),
        kt=vm((full, 256), BF),
        vt=vm((full, 256), BF),
        dgo=vm((2, full, 256), BF),
        mst=vm((3, full, 1), F32),
        lst=vm((3, full, 1), F32),
        attf=vm((2, full, 256), F32),
        attb=vm((2, 2, two, 256), BF),
        gl=vm((2, 2, two, ff), BF),
        gp=vm((2, 2, two, ff), F32),
        du=vm((2, two, ff), BF),
        dhb=vm((2, 2, two, dim), BF),
        dhf=vm((two, dim), F32),
        gm=vm((2, two, 640), BF),
        ma=vm((3, full, 256), BF),
        mb=vm((3, full, 256), BF),
        dqs=vm((full, 256), F32),
        dks=vm((full, 256), F32),
        dvs=vm((full, 256), F32),
        cs=vm((two, dim), BF),
        cr=vm((SLOTS, two, dim), BF),
        ys=vm((2, two, dim), BF),
        yr=vm((SLOTS, two, dim), BF),
        chip=vm((2, two, dim), F32),
        gr=vm((2, dim, wide), BF),
        ar=vm((2, half - 1, 2, part, wide), BF),
        bs=vm((2, part, wide), BF),
        br=vm((2, part, wide), BF),
        c2s=vm((part, wide), BF),
        c2r=vm((part, wide), BF),
        smo=vm((2, 8, dim), F32),
        smc=vm((2, 8, dim), F32),
        smr=vm((2 * nd - 1, 8, dim), F32),
        stt=vm((6, RB, dim), F32),
        oq=vm((4, rows, dim), BF),
        s_loc=dma((12,)),
        s_red=dma((4,)),
        s_xy=dma((4,)),
        s_wx=dma((2, 5)),
        s_wzs=dma((4, half)),
        s_wzr=dma((4, half)),
        s_ag=dma((2, 8)),
        s_cc=dma((2, SLOTS)),
        s_yy=dma((2, SLOTS)),
        s_kvs=dma((2, nd)),
        s_kvr=dma((2, nd)),
        s_qs=dma((2, nd)),
        s_qr=dma((2, nd)),
        s_ds=dma((2, nd)),
        s_dr=dma((2, nd)),
        s_as=dma((2, 4, half, 2)),
        s_ar=dma((2, 4, half, 2)),
        s_b=dma((2, 4)),
        s_c=dma((2, 4)),
        s_sm=dma((2,)),
        s_sms=dma((2 * nd - 1,)),
        s_smr=dma((2 * nd - 1,)),
        s_out=dma((4, 3)),
    )


def mega(nd, names, *refs):
    (fr, og, wq, wo, wu, wd, sp, kf, qf) = refs[:9]
    (acts, igs, o_q, o_u, o_o, o_d, o_s) = refs[9:16]
    b_ = dict(zip(names, refs[16:]))
    big = nd > MOST

    class Bufs:
        pass

    v = Bufs()
    v.__dict__.update(b_)
    half = nd // 2
    rows, dim = fr.shape[1:]
    two, full = 2 * rows, 4 * rows
    ff = wu.shape[1]
    part = dim // nd
    s = lax.axis_index("section")
    z = lax.axis_index("dp")
    t = lax.axis_index("tensor")
    g, zi = z // half, z % half
    c, y = t % 2, t // 2
    own_b = zi + half * s
    zo = (z + half) % nd
    me_x = (1 - s, z, t)
    me_c = (s, z, t + 1 - 2 * c)
    me_y = (s, z, (t + 2) % 4)
    me_o = (s, zo, t)

    def zpeer(d):
        return (s, g * half + (zi + d) % half, t)

    def member(k):
        zk, sk = (zi + k % half) % half, (s + k // half) % 2
        return (sk, g * half + zk, t), zk + half * sk

    def remote(src, dst, ss, rs, dev):
        return pltpu.make_async_remote_copy(
            src_ref=src, dst_ref=dst, send_sem=ss, recv_sem=rs, device_id=dev, device_id_type=MESH
        )

    late = []

    def send(src, dst, ss, rs, dev):
        cp = remote(src, dst, ss, rs, dev)
        cp.start()
        late.append(cp)
        return cp

    loads = [
        pltpu.make_async_copy(wq.at[pl.ds(0, 192)], v.wqb.at[s, pl.ds(0, 192)], v.s_loc.at[0]),
        pltpu.make_async_copy(wq.at[pl.ds(192, 384)], v.wqb.at[s, pl.ds(256, 384)], v.s_loc.at[1]),
        pltpu.make_async_copy(wo, v.wob.at[s, pl.ds(64, 192)], v.s_loc.at[2]),
        pltpu.make_async_copy(wu, v.wub.at[s], v.s_loc.at[3]),
        pltpu.make_async_copy(wd, v.wdb.at[s], v.s_loc.at[4]),
        pltpu.make_async_copy(sp, v.spb.at[s], v.s_loc.at[5]),
    ]
    for cp in loads:
        cp.start()
    v.wqb[s, pl.ds(192, 64), :] = jnp.zeros((64, dim), BF)
    v.wob[s, pl.ds(0, 64), :] = jnp.zeros((64, dim), BF)

    barrier = pltpu.get_barrier_semaphore()
    for k in range(1, 2 * nd):
        other = (s * nd + z + k) % (2 * nd)
        pl.semaphore_signal(barrier, inc=1, device_id=(other // nd, other % nd, t), device_id_type=MESH)
    for dev in (me_c, me_y):
        pl.semaphore_signal(barrier, inc=1, device_id=dev, device_id_type=MESH)
    pl.semaphore_wait(barrier, 2 * nd + 1)

    keeps = g == s

    def red(src, dst, i):
        @pl.when(keeps)
        def _():
            pltpu.make_async_copy(src.at[g], dst.at[0], v.s_loc.at[6 + i]).start()
            remote(src.at[1 - g], dst.at[0], v.s_red.at[i], v.s_red.at[2 + i], me_o).start()

    def red_wait(src, dst, i):
        @pl.when(keeps)
        def _():
            pltpu.make_async_copy(src.at[g], dst.at[0], v.s_loc.at[6 + i]).wait()

        @pl.when(jnp.logical_not(keeps))
        def _():
            remote(src.at[1 - g], dst.at[0], v.s_red.at[i], v.s_red.at[2 + i], me_o).wait_recv()

    red(fr, v.xq, 0)
    for cp in loads[:2]:
        cp.wait()
    loads[5].wait()
    mats = (v.wqb, v.wob, v.wub, v.wdb)

    def w_rows(i, p):
        n = mats[i].shape[1] // half
        return pl.ds(pl.multiple_of(p * n, 16), n)

    def ship(i):
        src = mats[i].at[s, w_rows(i, zi)]
        send(src, src, v.s_wx.at[0, i], v.s_wx.at[1, i], me_x)

    send(v.spb.at[s], v.spb.at[s], v.s_wx.at[0, 4], v.s_wx.at[1, 4], me_x)
    ship(0)
    loads[2].wait()
    ship(1)
    loads[3].wait()
    ship(2)
    loads[4].wait()
    ship(3)
    red(og, v.gq, 1)

    def forward_w(i):
        src = mats[i].at[1 - s, w_rows(i, zi)]
        remote(src, src, v.s_wx.at[0, i], v.s_wx.at[1, i], me_x).wait_recv()
        for d in range(1, half):
            send(src, src, v.s_wzs.at[i, d], v.s_wzr.at[i, d], zpeer(d))

    def gather_w(i, layer):
        @pl.when(s != layer)
        def _():
            for d in range(1, half):
                src = mats[i].at[1 - s, w_rows(i, (zi + half - d) % half)]
                remote(src, src, v.s_wzs.at[i, d], v.s_wzr.at[i, d], zpeer(d)).wait_recv()

    red_wait(fr, v.xq, 0)
    send(v.xq.at[0], v.xq.at[1], v.s_xy.at[0], v.s_xy.at[1], me_y)
    remote(v.spb.at[s], v.spb.at[s], v.s_wx.at[0, 4], v.s_wx.at[1, 4], me_x).wait_recv()
    q_own = pl.ds(pl.multiple_of(rows * y, 8), rows)
    q_oth = pl.ds(pl.multiple_of(rows * (1 - y), 8), rows)
    v.xres[q_own, :] = v.xq[0].astype(F32)
    remote(v.xq.at[0], v.xq.at[1], v.s_xy.at[0], v.s_xy.at[1], me_y).wait_recv()
    v.xres[q_oth, :] = v.xq[1].astype(F32)

    def prow(layer, i):
        return v.spb[layer, i : i + 1, :]

    def row_loop(fn, n=two):
        def step(i, carry):
            fn(pl.ds(pl.multiple_of(i * RB, RB), RB))
            return carry

        lax.fori_loop(0, n // RB, step, 0)

    def unit(x):
        cen = x - jnp.mean(x, axis=-1, keepdims=True)
        r = lax.rsqrt(jnp.mean(cen * cen, axis=-1, keepdims=True) + 1e-05)
        return cen * r, r

    def share(buf, layer, i):
        src = buf.at[layer, c]
        send(src, src, v.s_ag.at[0, i], v.s_ag.at[1, i], me_c)

    def share_wait(buf, layer, i):
        src = buf.at[layer, 1 - c]
        remote(src, src, v.s_ag.at[0, i], v.s_ag.at[1, i], me_c).wait_recv()

    def norm_one(layer):
        gain, shift = prow(layer, 0), prow(layer, 2)

        def body(rs):
            u, r = unit(v.xres[rs, :])
            v.u1[layer, rs, :] = u
            v.r1[layer, rs, :] = r
            v.nb[layer, c, rs, :] = (u * gain + shift).astype(BF)

        row_loop(body)
        share(v.nb, layer, layer)

    def sum_begin(j, term):
        k = j % SLOTS
        v.cs[...] = term(1 - c).astype(BF)
        cp = remote(v.cs, v.cr.at[k], v.s_cc.at[0, k], v.s_cc.at[1, k], me_c)
        cp.start()
        v.chip[j % 2] = term(c)
        cp.wait()

        def body(rs):
            tot = v.chip[j % 2, rs, :] + v.cr[k, rs, :].astype(F32)
            v.chip[j % 2, rs, :] = tot
            v.ys[j % 2, rs, :] = tot.astype(BF)

        row_loop(body)
        remote(v.ys.at[j % 2], v.yr.at[k], v.s_yy.at[0, k], v.s_yy.at[1, k], me_y).start()

    def sum_end(j):
        k = j % SLOTS
        remote(v.ys.at[j % 2], v.yr.at[k], v.s_yy.at[0, k], v.s_yy.at[1, k], me_y).wait()

    def sum_rows(j, rs):
        k = j % SLOTS
        return v.chip[j % 2, rs, :] + v.yr[k, rs, :].astype(F32)

    lane_f = lax.broadcasted_iota(jnp.int32, (full, 256), 1)
    lane = lax.broadcasted_iota(jnp.int32, (full, 128), 1)

    def k_mask(h):
        return (
            ((lane_f >= 64 * h) & (lane_f < 64 * h + 64))
            | ((lane_f >= 192 + 3 * h) & (lane_f < 195 + 3 * h))
            | (lane_f >= 208)
        )

    def v_mask(h):
        return ((lane_f >= 64 * h + 64) & (lane_f < 64 * h + 128)) | (
            (lane_f >= 3 * h) & (lane_f < 3 * h + 3)
        )

    def by_head_k(a):
        return jnp.where(lane_f < 64, a[0], jnp.where(lane_f < 128, a[1], a[2]))

    def by_head_v(a):
        return jnp.where(lane_f < 128, a[0], jnp.where(lane_f < 192, a[1], a[2]))

    def put_masked(dst, val, mask):
        val = val.astype(F32)
        for h in range(3):
            dst[h] = jnp.where(mask(h), val, 0.0).astype(BF)

    def build_kv(layer, bk):
        v.kt[:, 0:128] = v.kvb[layer, bk, :, 0:128]
        mid = v.kvb[layer, bk, :, 128:256].astype(F32)
        v.kt[:, 128:256] = jnp.where(lane < 64, mid, kf[bk].astype(F32)).astype(BF)
        v.vt[:, 0:128] = jnp.where(lane < 64, jnp.where(lane < 9, 1.0, 0.0), mid).astype(BF)
        v.vt[:, 128:256] = v.kvb[layer, bk, :, 256:384]

    def splits(x):
        hi = x.astype(BF).astype(F32)
        mid = (x - hi).astype(BF).astype(F32)
        return hi, mid, (x - hi) - mid

    def group_send(src, dst, ss, rs):
        for k in range(1, nd):
            dev, _ = member(k)
            send(src, dst, ss.at[k], rs.at[own_b], dev)

    def group_wait(buf, layer, rs, k, ss):
        dev, bk = member(k)
        dst = buf.at[layer, bk]
        remote(dst, dst, ss.at[0], rs.at[bk], dev).wait_recv()

    halves = (lambda i: c, lambda i: 1 - c)

    def forward(layer):
        bias_q, bias_kv = v.spb[layer, 7:8, 0:256], v.spb[layer, 8:9, 0:384]

        def qkv(hf):
            r = nt(v.nb[layer, hf], v.wqb[layer])
            rs = pl.ds(pl.multiple_of(hf * two, 16), two)
            q = (r[:, 0:256] + bias_q).astype(BF).astype(F32) * 0.125
            v.qa[layer, rs, 0:128] = q[:, 0:128].astype(BF)
            v.qa[layer, rs, 128:256] = (q[:, 128:256] + qf[rs, :].astype(F32)).astype(BF)
            v.kvb[layer, own_b, rs, :] = (r[:, 256:640] + bias_kv).astype(BF)

        if layer == 0:
            forward_w(0)
        gather_w(0, layer)
        qkv(c)
        share_wait(v.nb, layer, layer)
        qkv(1 - c)
        group_send(v.kvb.at[layer, own_b], v.kvb.at[layer, own_b], v.s_kvs.at[layer], v.s_kvr.at[layer])

        put_masked(v.ma, v.qa[layer], k_mask)
        v.mst[...] = jnp.full(v.mst.shape, -3e38, F32)
        v.lst[...] = jnp.zeros(v.lst.shape, F32)
        v.dqs[...] = jnp.zeros(v.dqs.shape, F32)

        def block(k, carry):
            zk, sk = (zi + k % half) % half, (s + k // half) % 2
            bk = zk + half * sk

            @pl.when(k > 0)
            def _():
                dst = v.kvb.at[layer, bk]
                remote(dst, dst, v.s_kvs.at[layer, 0], v.s_kvr.at[layer, bk], me_x).wait_recv()

            build_kv(layer, bk)
            kt, vt = v.kt[...], v.vt[...]
            alphas, news = [], []
            for h in range(3):
                sc = nt(v.ma[h], kt)
                old = v.mst[h]
                new = jnp.maximum(old, jnp.max(sc, axis=1, keepdims=True))
                alpha = jnp.exp(old - new)
                p = jnp.exp(sc - new)
                v.mst[h] = new
                v.lst[h] = v.lst[h] * alpha + jnp.sum(p, axis=1, keepdims=True)
                hi = p.astype(BF)
                lo = (p - hi.astype(F32)).astype(BF)
                news.append(nn(hi, vt) + nn(lo, vt))
                alphas.append(alpha)
            v.dqs[...] = v.dqs[...] * by_head_v(alphas) + by_head_v(news)
            return carry

        block(0, 0)
        if layer == 0:
            forward_w(1)
            forward_w(2)
        lax.fori_loop(1, nd, block, 0)

        att = v.dqs[...] * by_head_v([1.0 / v.lst[h] for h in range(3)])
        v.attf[layer] = att
        v.attb[layer] = att.astype(BF).reshape(2, two, 256)
        tile = v.qa[layer, :, 128:256].astype(F32)
        for h in range(3):
            for i, piece in enumerate(splits(-(v.mst[h] + jnp.log(v.lst[h])))):
                tile = jnp.where(lane == 64 + 3 * h + i, piece, tile)
        v.qa[layer, :, 128:256] = tile.astype(BF)
        if layer == 0:
            forward_w(3)
        gather_w(1, layer)
        sum_begin(2 * layer, lambda hf: nn(v.attb[layer, hf], v.wob[layer]))
        group_send(v.qa.at[layer], v.qg.at[layer, own_b], v.s_qs.at[layer], v.s_qr.at[layer])
        sum_end(2 * layer)
        out_bias, gain2, shift2 = prow(layer, 4), prow(layer, 1), prow(layer, 3)

        def body(rs):
            hid = v.xres[rs, :] + sum_rows(2 * layer, rs) + out_bias
            v.hid[rs, :] = hid
            u, r = unit(hid)
            v.u2[layer, rs, :] = u
            v.r2[layer, rs, :] = r
            v.sb[layer, c, rs, :] = (u * gain2 + shift2).astype(BF)

        row_loop(body)
        share(v.sb, layer, 2 + layer)
        gather_w(2, layer)
        bias_up = prow(layer, 6)

        def up(hf):
            v.gp[layer, hf] = nn(v.sb[layer, hf], v.wub[layer]) + bias_up

            def gelu(rs):
                u = v.gp[layer, hf, rs, :]
                phi = 0.5 * (1.0 + lax.erf(u * 0.7071067811865476))
                v.gl[layer, hf, rs, :] = (u * phi).astype(BF)
                v.gp[layer, hf, rs, :] = phi + u * (jnp.exp(-0.5 * u * u) * 0.3989422804014327)

            row_loop(gelu)

        up(c)
        share_wait(v.sb, layer, 2 + layer)
        up(1 - c)
        gather_w(3, layer)
        sum_begin(2 * layer + 1, lambda hf: nn(v.gl[layer, hf], v.wdb[layer]))

    def forward_end(layer):
        sum_end(2 * layer + 1)
        out_bias = prow(layer, 5)

        def body(rs):
            out = v.hid[rs, :] + sum_rows(2 * layer + 1, rs) + out_bias
            v.xres[rs, :] = out.astype(BF).astype(F32)

        row_loop(body)
        if layer == 0:
            norm_one(1)
        put_out(layer, layer, v.xres, acts)

    def put_out(i, layer, src, dst):
        v.oq[i] = src[q_own, :].astype(BF)
        here = keeps & (s == layer)

        @pl.when(here)
        def _():
            pltpu.make_async_copy(v.oq.at[i], dst.at[g], v.s_loc.at[8 + i]).start()

        @pl.when(jnp.logical_not(here))
        def _():
            remote(v.oq.at[i], dst.at[g], v.s_out.at[i, 0], v.s_out.at[i, 1 + g], (layer, own_b, t)).start()

    def put_out_wait(i, layer, dst):
        here = keeps & (s == layer)

        @pl.when(here)
        def _():
            pltpu.make_async_copy(v.oq.at[i], dst.at[g], v.s_loc.at[8 + i]).wait()

        @pl.when(jnp.logical_not(here))
        def _():
            remote(v.oq.at[i], dst.at[g], v.s_out.at[i, 0], v.s_out.at[i, 1 + g], (layer, own_b, t)).wait_send()

        @pl.when(s == layer)
        def _():
            def got(m):
                remote(v.oq.at[i], dst.at[m], v.s_out.at[i, 0], v.s_out.at[i, 1 + m], me_x).wait_recv()

            got(1 - g)

            @pl.when(g != s)
            def _():
                got(g)

    col = dict(d=0, u=ff, o=2 * ff, q=2 * ff + 256)
    width = dict(d=ff, u=ff, o=256, q=640)

    def grad_of(layer, key, left, right):
        o, n = col[key], width[key]
        for i in range(dim // 256):
            lo = i * 256
            v.gr[layer, lo : lo + 256, o : o + n] = tn(left[:, lo : lo + 256], right).astype(BF)
        i = "duoq".index(key)
        for d in range(1, half):
            zp = (zi + d) % half
            for k in range(2):
                rs = pl.ds(pl.multiple_of((zp + half * k) * part, 16), part)
                send(
                    v.gr.at[layer, rs, pl.ds(o, n)],
                    v.ar.at[layer, d - 1, k, :, pl.ds(o, n)],
                    v.s_as.at[layer, i, d, k],
                    v.s_ar.at[layer, i, d, k],
                    zpeer(d),
                )

    def rows_of(buf, layer):
        x = buf[layer]
        return x.reshape(full, x.shape[-1])

    def back_rows(layer, j, u_buf, r_buf, gain, base, at, extra=None):
        v.stt[...] = jnp.zeros(v.stt.shape, F32)

        def body(rs):
            gsec = sum_rows(j, rs)
            u, r = u_buf[layer, rs, :], r_buf[layer, rs, :]
            gg = gsec * gain
            res = r * (
                gg - jnp.mean(gg, axis=-1, keepdims=True) - u * jnp.mean(gg * u, axis=-1, keepdims=True)
            )
            inn = base[rs, :]
            out = inn + res
            at(rs, out)
            v.stt[0] += gsec * u
            v.stt[1] += gsec
            v.stt[2] += out
            v.stt[3] += inn

        row_loop(body)

    def backward_begin(layer):
        def d_second(hf):
            dgel = nt(v.dyb[layer, hf], v.wdb[layer])
            v.du[hf] = (dgel * v.gp[layer, hf]).astype(BF)
            return nt(v.du[hf], v.wub[layer])

        sum_begin(4 + 2 * (1 - layer), d_second)

    def backward(layer):
        j = 4 + 2 * (1 - layer)
        grad_of(layer, "d", rows_of(v.dyb, layer), rows_of(v.gl, layer))
        grad_of(layer, "u", rows_of(v.sb, layer), v.du[...].reshape(full, ff))
        ones = jnp.ones((8, full), BF)
        v.smo[layer, 6:7, :] = nn(ones, v.du[...].reshape(full, ff))[0:1]
        sum_end(j)

        def at_two(rs, out):
            v.dhf[rs, :] = out
            v.dhb[layer, c, rs, :] = out.astype(BF)

        back_rows(layer, j, v.u2, v.r2, prow(layer, 1), v.dyf, at_two)
        share(v.dhb, layer, 4 + layer)
        for i, row in ((0, 1), (1, 3), (2, 4), (3, 5)):
            v.smo[layer, row : row + 1, :] = jnp.sum(v.stt[i], axis=0, keepdims=True)

        def d_att(hf):
            rs = pl.ds(pl.multiple_of(hf * two, 16), two)
            v.dgo[layer, rs, :] = nt(v.dhb[layer, hf], v.wob[layer]).astype(BF)

        d_att(c)
        share_wait(v.dhb, layer, 4 + layer)
        d_att(1 - c)
        dat = v.dgo[layer].astype(F32)
        prod = dat * v.attf[layer]
        tile = dat[:, 0:128]
        for h in range(3):
            real = (lane_f >= 64 * h + 64) & (lane_f < 64 * h + 128)
            delta = jnp.sum(jnp.where(real, prod, 0.0), axis=1, keepdims=True)
            for i, piece in enumerate(splits(-delta)):
                tile = jnp.where(lane == 3 * h + i, piece, tile)
        v.dgo[layer, :, 0:128] = tile.astype(BF)
        group_send(v.dgo.at[layer], v.dg.at[layer, own_b], v.s_ds.at[layer], v.s_dr.at[layer])
        grad_of(layer, "o", rows_of(v.dhb, layer), rows_of(v.attb, layer))

        put_masked(v.ma, v.qa[layer], k_mask)
        put_masked(v.mb, v.dgo[layer], v_mask)
        v.dqs[...] = jnp.zeros(v.dqs.shape, F32)

        def query_block(bk, carry):
            build_kv(layer, bk)
            kt, vt = v.kt[...], v.vt[...]
            terms = []
            for h in range(3):
                p = jnp.exp(nt(v.ma[h], kt))
                ds = (p * nt(v.mb[h], vt)).astype(BF)
                terms.append(nn(ds, kt))
            v.dqs[...] += by_head_k(terms)
            return carry

        lax.fori_loop(0, nd, query_block, 0)

        build_kv(layer, own_b)
        put_masked(v.ma, v.kt[...], k_mask)
        put_masked(v.mb, v.vt[...], v_mask)
        v.dks[...] = jnp.zeros(v.dks.shape, F32)
        v.dvs[...] = jnp.zeros(v.dvs.shape, F32)

        def key_block(k, carry):
            zk, sk = (zi + k % half) % half, (s + k // half) % 2
            bk = zk + half * sk
            q_at, d_at = v.qg.at[layer, bk], v.dg.at[layer, bk]
            remote(q_at, q_at, v.s_qs.at[layer, 0], v.s_qr.at[layer, bk], me_x).wait_recv()
            remote(d_at, d_at, v.s_ds.at[layer, 0], v.s_dr.at[layer, bk], me_x).wait_recv()
            if big:
                cps = (
                    pltpu.make_async_copy(q_at, v.kt, v.s_loc.at[0]),
                    pltpu.make_async_copy(d_at, v.vt, v.s_loc.at[1]),
                )
                for cp in cps:
                    cp.start()
                for cp in cps:
                    cp.wait()
                key_terms(v.kt[...], v.vt[...])
            else:
                key_terms(q_at[...], d_at[...])
            return carry

        def key_terms(qt, dt):
            tk, tv = [], []
            for h in range(3):
                p = jnp.exp(nt(v.ma[h], qt))
                ds = (p * nt(v.mb[h], dt)).astype(BF)
                tv.append(nn(p.astype(BF), dt))
                tk.append(nn(ds, qt))
            v.dks[...] += by_head_k(tk)
            v.dvs[...] += by_head_v(tv)

        key_terms(v.qa[layer], v.dgo[layer])
        lax.fori_loop(1, nd, key_block, 0)

        for i in range(2):
            rs = slice(i * two, (i + 1) * two)
            v.gm[i, :, 0:128] = (v.dqs[rs, 0:128] * 0.125).astype(BF)
            v.gm[i, :, 128:256] = jnp.where(lane[rs] < 64, v.dqs[rs, 128:256] * 0.125, 0.0).astype(BF)
            v.gm[i, :, 256:384] = v.dks[rs, 0:128].astype(BF)
            v.gm[i, :, 384:512] = jnp.where(lane[rs] < 64, v.dks[rs, 128:256], v.dvs[rs, 0:128]).astype(BF)
            v.gm[i, :, 512:640] = v.dvs[rs, 128:256].astype(BF)
        sum_begin(j + 1, lambda hf: nn(v.gm[hf], v.wqb[layer]))
        grad_of(layer, "q", rows_of(v.nb, layer), v.gm[...].reshape(full, 640))
        v.smo[layer, 7:8, :] = jnp.zeros((1, dim), F32)
        v.smo[layer, 7:8, 0:640] = nn(ones, v.gm[...].reshape(full, 640))[0:1]
        sum_end(j + 1)

        def at_one(rs, out):
            low = out.astype(BF)
            v.dyf[rs, :] = low.astype(F32)
            if layer == 1:
                v.dyb[0, c, rs, :] = low

        back_rows(layer, j + 1, v.u1, v.r1, prow(layer, 0), v.dhf, at_one)
        for i, row in ((0, 0), (1, 2)):
            v.smo[layer, row : row + 1, :] = jnp.sum(v.stt[i], axis=0, keepdims=True)
        if layer == 1:
            share(v.dyb, 0, 7)
        put_out(2 + layer, layer, v.dyf, igs)

    norm_one(0)
    forward(0)
    forward_end(0)
    red_wait(og, v.gq, 1)
    send(v.gq.at[0], v.gq.at[1], v.s_xy.at[2], v.s_xy.at[3], me_y)
    forward(1)
    v.dyf[q_own, :] = v.gq[0].astype(F32)
    remote(v.gq.at[0], v.gq.at[1], v.s_xy.at[2], v.s_xy.at[3], me_y).wait_recv()
    v.dyf[q_oth, :] = v.gq[1].astype(F32)
    v.dyb[1, c] = v.dyf[...].astype(BF)
    share(v.dyb, 1, 6)
    share_wait(v.dyb, 1, 6)
    backward_begin(1)
    forward_end(1)
    backward(1)
    share_wait(v.dyb, 0, 7)
    backward_begin(0)
    backward(0)

    for layer in (1, 0):
        for i in range(4):
            key = "duoq"[i]
            for d in range(1, half):
                for k in range(2):
                    dst = v.ar.at[layer, d - 1, k, :, pl.ds(col[key], width[key])]
                    remote(dst, dst, v.s_as.at[layer, i, d, k], v.s_ar.at[layer, i, d, k], zpeer(d)).wait_recv()

    def pair_sum(layer, k, rs):
        own = pl.ds(pl.multiple_of((zi + half * k) * part + rs.start, 16), RB)
        tot = v.gr[layer, own, :].astype(F32)
        for d in range(1, half):
            tot = tot + v.ar[layer, d - 1, k, rs, :].astype(F32)
        return tot

    for k in range(2):

        def send_rows(rs, k=k):
            v.bs[k, rs, :] = pair_sum(1 - s, k, rs).astype(BF)

        row_loop(send_rows, part)
        send(v.bs.at[k], v.br.at[k], v.s_b.at[0, k], v.s_b.at[1, k], me_x)
    send(v.smo, v.smc, v.s_sm.at[0], v.s_sm.at[1], me_c).wait_recv()
    for layer in range(2):
        rowid = lax.broadcasted_iota(jnp.int32, (8, dim), 0)
        v.smc[layer] = v.smo[layer] + jnp.where(rowid < 6, v.smc[layer], 0.0)
    for k in range(1, 2 * nd):
        other = (s * nd + z + k) % (2 * nd)
        so = other // nd
        send(v.smc.at[so], v.smr.at[k - 1], v.s_sms.at[k - 1], v.s_smr.at[k - 1], (so, other % nd, t))

    def put(rs, tot):
        for o_ref, key in ((o_d, "d"), (o_u, "u"), (o_o, "o"), (o_q, "q")):
            o_ref[rs, :] = tot[:, col[key] : col[key] + width[key]]

    for k in (1, 0):
        kk = (g + k) % 2
        remote(v.bs.at[kk], v.br.at[kk], v.s_b.at[0, kk], v.s_b.at[1, kk], me_x).wait_recv()

        def add_rows(rs, k=k, kk=kk):
            tot = pair_sum(s, kk, rs) + v.br[kk, rs, :].astype(F32)
            if k == 1:
                v.c2s[rs, :] = tot.astype(BF)
            else:
                put(rs, tot)

        row_loop(add_rows, part)
        if k == 1:
            send(v.c2s, v.c2r, v.s_c.at[0, 0], v.s_c.at[1, 0], me_o)
    for k in range(1, 2 * nd):
        remote(v.smr.at[0], v.smr.at[k - 1], v.s_sms.at[k - 1], v.s_smr.at[k - 1], me_x).wait_recv()
    tot = v.smc[s]
    for k in range(1, 2 * nd):
        tot = tot + v.smr[k - 1]
    o_s[...] = tot
    remote(v.c2s, v.c2r, v.s_c.at[0, 0], v.s_c.at[1, 0], me_o).wait_recv()

    def last_rows(rs):
        for o_ref, key in ((o_d, "d"), (o_u, "u"), (o_o, "o"), (o_q, "q")):
            o_ref[rs, :] += v.c2r[rs, col[key] : col[key] + width[key]].astype(F32)

    row_loop(last_rows, part)

    for cp in late:
        cp.wait_send()
    for i, src, dst in ((0, fr, v.xq), (1, og, v.gq)):

        @pl.when(keeps)
        def _(i=i, src=src, dst=dst):
            remote(src.at[1 - g], dst.at[0], v.s_red.at[i], v.s_red.at[2 + i], me_o).wait_send()

    put_out_wait(0, 0, acts)
    put_out_wait(1, 1, acts)
    put_out_wait(2, 0, igs)
    put_out_wait(3, 1, igs)


def local(frames, out_grad, clip_ids, w_qkv, bias_qv, w_out, w_up, bias_up, w_down, ln_gain, shifts):
    rows, dim = frames.shape[1:]
    nd = lax.axis_size("dp")
    half = nd // 2
    z, t, s = lax.axis_index("dp"), lax.axis_index("tensor"), lax.axis_index("section")
    hl = w_qkv.shape[3]
    ff = w_up.shape[2]
    part = dim // nd
    wide = w_qkv[0].transpose(1, 2, 0).reshape(3 * hl, dim)
    zeros = functools.partial(jnp.zeros, dtype=F32)
    params = jnp.concatenate(
        [
            ln_gain[0].astype(F32),
            shifts[0].astype(F32),
            bias_up.astype(F32),
            jnp.pad(bias_qv[0, 0].astype(F32), (0, dim - hl))[None],
            jnp.pad(bias_qv[0, 1].astype(F32), (hl, dim - 2 * hl))[None],
            zeros((7, dim)),
        ]
    )
    clip = lax.dynamic_index_in_dim(clip_ids, z // half, 0, keepdims=False)
    clip = clip.reshape(nd, 4, rows)
    clip = jnp.stack([clip[:, 0], clip[:, 2], clip[:, 1], clip[:, 3]], axis=1).reshape(nd, 4 * rows)
    lane = jnp.arange(128)
    same = clip[:, :, None] == (lane - 80)[None, None, :]
    spot = lane >= 80
    k_feat = jnp.where(
        (lane >= 64) & (lane < 73), 1.0, jnp.where(spot & jnp.logical_not(same), -BIG, 0.0)
    ).astype(BF)
    own_b = z % half + half * s
    q_feat = jnp.where(spot & lax.dynamic_index_in_dim(same, own_b, 0, keepdims=False), 1.0, 0.0).astype(BF)

    plan = scratch_plan(nd, rows, dim, hl, ff)
    shape = jax.ShapeDtypeStruct
    anyspec = pl.BlockSpec(memory_space=pl.ANY)
    vspec = pl.BlockSpec(memory_space=pltpu.VMEM)
    gathered = {name: (2, nd, 4 * rows, 256) for name in ("qg", "dg")}
    big = nd > MOST
    if not big:
        plan.update({name: pltpu.VMEM(dims, BF) for name, dims in gathered.items()})
    outs = pl.pallas_call(
        functools.partial(mega, nd, (*gathered, *plan) if big else tuple(plan)),
        out_shape=(
            shape((2, rows, dim), BF),
            shape((2, rows, dim), BF),
            shape((part, 640), F32),
            shape((part, ff), F32),
            shape((part, 256), F32),
            shape((part, ff), F32),
            shape((8, dim), F32),
        )
        + tuple(shape(dims, BF) for dims in gathered.values()) * big,
        in_specs=[anyspec] * 7 + [vspec] * 2,
        out_specs=(anyspec,) * 2 + (vspec,) * 5 + (anyspec,) * (2 * big),
        scratch_shapes=list(plan.values()),
        compiler_params=pltpu.CompilerParams(
            collective_id=0, has_side_effects=True, vmem_limit_bytes=63 * 1024 * 1024
        ),
    )(frames, out_grad, wide, w_out[0], w_up[0], w_down[0], params, k_feat, q_feat)

    acts, igs, g_q, g_u, g_o, g_d, small = outs[:7]
    g_qkv = jnp.stack([g_q[:, 0:hl], g_q[:, 256 : 256 + hl], g_q[:, 256 + hl : 256 + 2 * hl]], axis=1)
    bias = small[7]
    bias = jnp.stack([bias[0:hl], bias[256 + hl : 256 + 2 * hl]]).reshape(2, hl // HD, HD)
    bias = lax.dynamic_slice_in_dim(bias, z * (HD // nd), HD // nd, 2)
    upb = small[6].reshape(hl // HD, ff // (hl // HD))
    upb = lax.dynamic_slice_in_dim(upb, z * (upb.shape[1] // nd), upb.shape[1] // nd, 1)
    own = dim // (4 * nd)
    norms = lax.dynamic_slice_in_dim(small, (z * 4 + t) * own, own, 1)
    return (
        acts[None],
        igs[None],
        g_qkv[None],
        bias[None],
        g_o[:, 64 : 64 + hl].T[None],
        g_u[None],
        upb[None],
        g_d.T[None],
        norms[None, 0:2],
        norms[None, 2:6],
    )


def solution(mesh):
    in_specs = (
        P(None, ("dp", "tensor"), None),
        P(None, ("dp", "tensor"), None),
        P(),
        P("section", None, None, "tensor"),
        P("section", None, "tensor"),
        P("section", "tensor", None),
        P("section", None, "tensor"),
        P("section", "tensor"),
        P("section", "tensor", None),
        P("section", None, None),
        P("section", None, None),
    )
    out_specs = (
        P("section", None, ("dp", "tensor"), None),
        P("section", None, ("dp", "tensor"), None),
        P("section", "dp", None, "tensor"),
        P("section", None, "tensor", "dp"),
        P("section", "tensor", "dp"),
        P("section", "dp", "tensor"),
        P("section", "tensor", "dp"),
        P("section", "tensor", "dp"),
        P("section", None, ("dp", "tensor")),
        P("section", None, ("dp", "tensor")),
    )
    return jax.shard_map(local, mesh=mesh, in_specs=in_specs, out_specs=out_specs, check_vma=False)
```

time: 1210 us -> 349 us (0.29)
  the two profiles are of different devices: /device:TPU:0 before, /device:TPU:24 now
where the time goes in v1:
time: 349 us; the launch traced here: 348 us
  Pallas kernels  330 us (95%)
  local copies, waits for them, and re-layouts  12.9 us (4%)
  other arithmetic  4.34 us (1%)
    pallas_call x1, Pallas kernels, local(): pl.pallas_call(functools.partial(mega, nd, (*gathered, *plan) if big else...  330 us

profile of v1, /device:TPU:24, one launch (start us, length us, event | category | flops | bytes accessed | tf_op | source)
XLA Modules:
  0.0 348.3 jit_solution(17579552855221192916)
XLA Ops:
  0.6 0.0 copy-start
  0.7 0.8 slice_reduce_fusion.3
  1.5 0.7 bitcast_convert_fusion.1
  2.2 0.1 pad_convert_fusion
  2.3 0.0 copy-done
  2.3 0.1 reshape.56
  2.4 0.1 eq.17
  2.5 0.7 bitcast_convert_fusion
  3.2 1.9 concatenate.4.refs_6_
  5.2 0.3 broadcast_compare_fusion
  5.4 0.7 select_convert_fusion.1.refs_8_
  6.1 1.0 select_convert_fusion.refs_7_
  7.1 330.3 %shard_map.186 = (bf16[2,88,768]{2,1,0:T(8,128)(2,1)}, bf16[2,88,768]{2,1,0:T(8,128)(2,1)}, f32[192,640]{1,0:T(8,128)}, f32[192,768]{1,0:T(8,128)}, f32[192,256]...) custom-call(bf16[2,88,768]{2,1,0:T(8,128)(2,1)} %refs_0_.1, bf16[2,88,768]{2,1,0:T(8,128)(2,1)} %refs_1_.1, ...), custom_call_target="tpu_custom_call" | custom-call | tf_op jit(solution)/shard_map/pallas_call | solution.py:818
  337.4 0.0 copy-start.1
  337.4 0.9 slice_reduce_fusion.2
  338.3 0.1 stack.29
  338.3 0.1 stack.30
  338.4 0.1 dynamic-slice_maximum_fusion
  338.5 0.6 copy.27
  339.1 0.8 constant_dynamic-slice_fusion
  339.9 0.8 slice_reduce_fusion
  340.6 0.1 constant_dynamic-slice_fusion.1
  340.7 0.6 broadcast_in_dim.89
  341.3 0.6 slice_bitcast_fusion.5
  341.8 0.6 slice_bitcast_fusion.4
  342.4 1.0 slice_bitcast_fusion
  343.4 0.8 copy.25
  344.2 0.0 copy-done.1
  344.2 0.0 copy-start.5
  344.3 0.0 copy-start.4
  344.3 0.1 slice_bitcast_fusion.3
  344.4 0.0 copy-start.3
  344.4 0.9 maximum_bitcast_fusion
  345.2 0.0 copy-done.5
  345.2 0.0 copy-start.2
  345.2 0.7 copy.32
  345.9 0.0 copy-done.4
  345.9 0.7 copy.33
  346.7 0.0 copy-done.3
  346.7 0.8 copy.34
  347.5 0.0 copy-done.2
  347.5 0.8 copy.35
  (9 shorter events, 0.1 us)
Async XLA Ops:
  0.6 1.6 copy-start
  337.4 6.9 %copy-start.1 = (f32[192,640]{1,0:T(8,128)S(1)}, f32[192,640]{1,0:T(8,128)}, u32[]{:S(2)}) copy-start(f32[192,640]{1,0:T(8,128)} %get-tuple-element.19) | copy-start | bytes 1474564
  344.2 1.0 copy-start.5
  344.3 1.7 copy-start.4
  344.4 2.3 copy-start.3
  345.2 2.2 copy-start.2

commit v2 on v1

--- a/solution.py
+++ b/solution.py
@@ -29,6 +29,27 @@
     return lax.dot_general(a, b, (((0,), (0,)), ((), ())), preferred_element_type=F32)
 
 
+def shares(key, ff):
+    return {
+        "d": (0, ff, ff // 2, ff // 2),
+        "u": (ff, ff, ff // 2, ff // 2),
+        "o": (2 * ff, 256, 128, 128),
+        "q": (2 * ff + 256, 640, 256, 384),
+    }[key]
+
+
+MODES = {
+    (1, "d"): "swap",
+    (1, "u"): "run",
+    (1, "o"): "swap",
+    (1, "q"): "swap",
+    (0, "d"): "run",
+    (0, "u"): "swap",
+    (0, "o"): "swap",
+    (0, "q"): "swap",
+}
+
+
 def scratch_plan(nd, rows, dim, head_dim, ff):
     half = nd // 2
     full = 4 * rows
@@ -37,7 +58,7 @@
     wide = 640 + ff + 256 + ff
     vm = pltpu.VMEM
     dma = pltpu.SemaphoreType.DMA
-    return dict(
+    plan = dict(
         wqb=vm((2, 640, dim), BF),
         wob=vm((2, 256, dim), BF),
         wub=vm((2, dim, ff), BF),
@@ -81,11 +102,6 @@
         yr=vm((SLOTS, two, dim), BF),
         chip=vm((2, two, dim), F32),
         gr=vm((2, dim, wide), BF),
-        ar=vm((2, half - 1, 2, part, wide), BF),
-        bs=vm((2, part, wide), BF),
-        br=vm((2, part, wide), BF),
-        c2s=vm((part, wide), BF),
-        c2r=vm((part, wide), BF),
         smo=vm((2, 8, dim), F32),
         smc=vm((2, 8, dim), F32),
         smr=vm((2 * nd - 1, 8, dim), F32),
@@ -94,9 +110,9 @@
         s_loc=dma((12,)),
         s_red=dma((4,)),
         s_xy=dma((4,)),
-        s_wx=dma((2, 5)),
-        s_wzs=dma((4, half)),
-        s_wzr=dma((4, half)),
+        s_wx=dma((2, 9)),
+        s_wzs=dma((8, half)),
+        s_wzr=dma((8, half)),
         s_ag=dma((2, 8)),
         s_cc=dma((2, SLOTS)),
         s_yy=dma((2, SLOTS)),
@@ -106,15 +122,31 @@
         s_qr=dma((2, nd)),
         s_ds=dma((2, nd)),
         s_dr=dma((2, nd)),
-        s_as=dma((2, 4, half, 2)),
-        s_ar=dma((2, 4, half, 2)),
-        s_b=dma((2, 4)),
-        s_c=dma((2, 4)),
         s_sm=dma((2,)),
         s_sms=dma((2 * nd - 1,)),
         s_smr=dma((2 * nd - 1,)),
         s_out=dma((4, 3)),
     )
+    for (layer, key), mode in MODES.items():
+        n = shares(key, ff)[1 if mode == "run" else 3]
+        tag = f"{layer}{key}"
+        if mode == "swap":
+            plan["xr" + tag] = vm((dim, n), BF)
+            plan["s_x" + tag] = dma((2,))
+        else:
+            plan["bs" + tag] = vm((2, part, n), BF)
+            plan["br" + tag] = vm((2, part, n), BF)
+            plan["s_b" + tag] = dma((2,))
+        plan["ar" + tag] = vm((half - 1, 2, part, n), BF)
+        plan["s_a" + tag] = dma((2, half, 2))
+        plan["cs" + tag] = vm((part, n), BF)
+        plan["cr" + tag] = vm((part, n), BF)
+        plan["s_c" + tag] = dma((2,))
+        if mode == "swap":
+            plan["es" + tag] = vm((part, n), BF)
+            plan["er" + tag] = vm((part, n), BF)
+            plan["s_e" + tag] = dma((2,))
+    return plan
 
 
 def mega(nd, names, *refs):
@@ -209,43 +241,58 @@
     loads[5].wait()
     mats = (v.wqb, v.wob, v.wub, v.wdb)
 
-    def w_rows(i, p):
+    def w_parts(i):
+        return 2 if mats[i].shape[1] // half % 32 == 0 else 1
+
+    def w_rows(i, p, e):
         n = mats[i].shape[1] // half
-        return pl.ds(pl.multiple_of(p * n, 16), n)
+        m = n // w_parts(i)
+        return pl.ds(pl.multiple_of(p * n + e * m, 16), m)
 
     def ship(i):
-        src = mats[i].at[s, w_rows(i, zi)]
-        send(src, src, v.s_wx.at[0, i], v.s_wx.at[1, i], me_x)
-
-    send(v.spb.at[s], v.spb.at[s], v.s_wx.at[0, 4], v.s_wx.at[1, 4], me_x)
+        for e in range(w_parts(i)):
+            src = mats[i].at[s, w_rows(i, zi, e)]
+            send(src, src, v.s_wx.at[0, 2 * i + e], v.s_wx.at[1, 2 * i + e], me_x)
+
+    send(v.spb.at[s], v.spb.at[s], v.s_wx.at[0, 8], v.s_wx.at[1, 8], me_x)
     ship(0)
     loads[2].wait()
     ship(1)
     loads[3].wait()
     ship(2)
     loads[4].wait()
-    ship(3)
-    red(og, v.gq, 1)
-
-    def forward_w(i):
-        src = mats[i].at[1 - s, w_rows(i, zi)]
-        remote(src, src, v.s_wx.at[0, i], v.s_wx.at[1, i], me_x).wait_recv()
-        for d in range(1, half):
-            send(src, src, v.s_wzs.at[i, d], v.s_wzr.at[i, d], zpeer(d))
+
+    def w_copy(i, e, d, back=0):
+        src = mats[i].at[1 - s, w_rows(i, (zi + back) % half, e)]
+        return remote(src, src, v.s_wzs.at[2 * i + e, d], v.s_wzr.at[2 * i + e, d], zpeer(d))
+
+    def forward_w(i, e=None):
+        for e in range(w_parts(i)) if e is None else (e,):
+            if e < w_parts(i):
+                src = mats[i].at[1 - s, w_rows(i, zi, e)]
+                remote(src, src, v.s_wx.at[0, 2 * i + e], v.s_wx.at[1, 2 * i + e], me_x).wait_recv()
+                for d in range(1, half):
+                    w_copy(i, e, d).start()
+
+    def forward_w_end(i):
+        for e in range(w_parts(i)):
+            for d in range(1, half):
+                w_copy(i, e, d).wait_send()
 
     def gather_w(i, layer):
         @pl.when(s != layer)
         def _():
-            for d in range(1, half):
-                src = mats[i].at[1 - s, w_rows(i, (zi + half - d) % half)]
-                remote(src, src, v.s_wzs.at[i, d], v.s_wzr.at[i, d], zpeer(d)).wait_recv()
+            for e in range(w_parts(i)):
+                for d in range(1, half):
+                    w_copy(i, e, d, half - d).wait_recv()
 
     red_wait(fr, v.xq, 0)
     send(v.xq.at[0], v.xq.at[1], v.s_xy.at[0], v.s_xy.at[1], me_y)
-    remote(v.spb.at[s], v.spb.at[s], v.s_wx.at[0, 4], v.s_wx.at[1, 4], me_x).wait_recv()
+    remote(v.spb.at[s], v.spb.at[s], v.s_wx.at[0, 8], v.s_wx.at[1, 8], me_x).wait_recv()
     q_own = pl.ds(pl.multiple_of(rows * y, 8), rows)
     q_oth = pl.ds(pl.multiple_of(rows * (1 - y), 8), rows)
     v.xres[q_own, :] = v.xq[0].astype(F32)
+    forward_w(0, 0)
     remote(v.xq.at[0], v.xq.at[1], v.s_xy.at[0], v.s_xy.at[1], me_y).wait_recv()
     v.xres[q_oth, :] = v.xq[1].astype(F32)
 
@@ -370,7 +417,7 @@
             v.kvb[layer, own_b, rs, :] = (r[:, 256:640] + bias_kv).astype(BF)
 
         if layer == 0:
-            forward_w(0)
+            forward_w(0, 1)
         gather_w(0, layer)
         qkv(c)
         share_wait(v.nb, layer, layer)
@@ -390,6 +437,13 @@
             def _():
                 dst = v.kvb.at[layer, bk]
                 remote(dst, dst, v.s_kvs.at[layer, 0], v.s_kvr.at[layer, bk], me_x).wait_recv()
+
+            if layer == 0:
+                for i in (1, 2):
+
+                    @pl.when(k == i)
+                    def _(i=i):
+                        forward_w(i)
 
             build_kv(layer, bk)
             kt, vt = v.kt[...], v.vt[...]
@@ -411,8 +465,7 @@
 
         block(0, 0)
         if layer == 0:
-            forward_w(1)
-            forward_w(2)
+            ship(3)
         lax.fori_loop(1, nd, block, 0)
 
         att = v.dqs[...] * by_head_v([1.0 / v.lst[h] for h in range(3)])
@@ -423,11 +476,13 @@
             for i, piece in enumerate(splits(-(v.mst[h] + jnp.log(v.lst[h])))):
                 tile = jnp.where(lane == 64 + 3 * h + i, piece, tile)
         v.qa[layer, :, 128:256] = tile.astype(BF)
-        if layer == 0:
-            forward_w(3)
         gather_w(1, layer)
         sum_begin(2 * layer, lambda hf: nn(v.attb[layer, hf], v.wob[layer]))
-        group_send(v.qa.at[layer], v.qg.at[layer, own_b], v.s_qs.at[layer], v.s_qr.at[layer])
+        if layer == 1:
+            for one in (1, 0):
+                group_send(v.qa.at[one], v.qg.at[one, own_b], v.s_qs.at[one], v.s_qr.at[one])
+        if layer == 0:
+            forward_w(3, 0)
         sum_end(2 * layer)
         out_bias, gain2, shift2 = prow(layer, 4), prow(layer, 1), prow(layer, 3)
 
@@ -441,6 +496,8 @@
 
         row_loop(body)
         share(v.sb, layer, 2 + layer)
+        if layer == 0:
+            forward_w(3, 1)
         gather_w(2, layer)
         bias_up = prow(layer, 6)
 
@@ -508,30 +565,209 @@
             def _():
                 got(g)
 
-    col = dict(d=0, u=ff, o=2 * ff, q=2 * ff + 256)
-    width = dict(d=ff, u=ff, o=256, q=640)
-
     def grad_of(layer, key, left, right):
-        o, n = col[key], width[key]
+        first, n = shares(key, ff)[:2]
         for i in range(dim // 256):
             lo = i * 256
-            v.gr[layer, lo : lo + 256, o : o + n] = tn(left[:, lo : lo + 256], right).astype(BF)
-        i = "duoq".index(key)
+            v.gr[layer, lo : lo + 256, first : first + n] = tn(left[:, lo : lo + 256], right).astype(BF)
+
+    def buf(name, layer, key):
+        return b_[f"{name}{layer}{key}"]
+
+    def swaps(layer, key):
+        return MODES[layer, key] == "swap"
+
+    def all_cols(key):
+        return pl.ds(*shares(key, ff)[:2])
+
+    def share_cols(key, e):
+        first, _, stride, n = shares(key, ff)
+        return pl.ds(pl.multiple_of(first + e * stride, 128), n)
+
+    def slice_rows(k, d=0):
+        return pl.multiple_of(((zi + d) % half + half * k) * part, 16)
+
+    def swap_copy(layer, key):
+        sem = buf("s_x", layer, key)
+        return remote(
+            v.gr.at[layer, :, share_cols(key, 1 - s)], buf("xr", layer, key), sem.at[0], sem.at[1], me_x
+        )
+
+    def run_copy(layer, key, d, k):
+        sem, rs = buf("s_a", layer, key), pl.ds(slice_rows(k, d), part)
+        if swaps(layer, key):
+            src = buf("xr", layer, key).at[rs]
+        else:
+            src = v.gr.at[layer, rs, all_cols(key)]
+        return remote(src, buf("ar", layer, key).at[d - 1, k], sem.at[0, d, k], sem.at[1, d, k], zpeer(d))
+
+    def run_copies(layer, key):
+        return [run_copy(layer, key, d, k) for d in range(1, half) for k in range(2)]
+
+    def cross_copy(layer, key):
+        sem = buf("s_b", layer, key)
+        return remote(buf("bs", layer, key), buf("br", layer, key), sem.at[0], sem.at[1], me_x)
+
+    def last_copy(layer, key):
+        sem = buf("s_c", layer, key)
+        return remote(buf("cs", layer, key), buf("cr", layer, key), sem.at[0], sem.at[1], me_o)
+
+    def home_copy(layer, key):
+        sem = buf("s_e", layer, key)
+        return remote(buf("es", layer, key), buf("er", layer, key), sem.at[0], sem.at[1], me_x)
+
+    def run_sum(layer, key, k, rs):
+        own = pl.ds(pl.multiple_of(slice_rows(k) + rs.start, 16), RB)
+        if swaps(layer, key):
+            tot = buf("xr", layer, key)[own, :].astype(F32)
+        else:
+            tot = v.gr[layer, own, all_cols(key)].astype(F32)
         for d in range(1, half):
-            zp = (zi + d) % half
+            tot = tot + buf("ar", layer, key)[d - 1, k, rs, :].astype(F32)
+        return tot
+
+    def out_of(key, e=0):
+        _, n, stride, m = shares(key, ff)
+        return dict(d=o_d, u=o_u, o=o_o, q=o_q)[key], e * stride
+
+    def give(layer, key):
+        if swaps(layer, key):
+            swap_copy(layer, key).start()
+        else:
+            for cp in run_copies(layer, key):
+                cp.start()
+
+    def second(layer, key):
+        if swaps(layer, key):
+            swap_copy(layer, key).wait_recv()
+            xr = buf("xr", layer, key)
+
+            def body(rs):
+                xr[rs, :] = (v.gr[layer, rs, share_cols(key, s)].astype(F32) + xr[rs, :].astype(F32)).astype(BF)
+
+            row_loop(body, dim)
+            for cp in run_copies(layer, key):
+                cp.start()
+            return
+
+        for cp in run_copies(layer, key):
+            cp.wait_recv()
+
+        @pl.when(s != layer)
+        def _():
             for k in range(2):
-                rs = pl.ds(pl.multiple_of((zp + half * k) * part, 16), part)
-                send(
-                    v.gr.at[layer, rs, pl.ds(o, n)],
-                    v.ar.at[layer, d - 1, k, :, pl.ds(o, n)],
-                    v.s_as.at[layer, i, d, k],
-                    v.s_ar.at[layer, i, d, k],
-                    zpeer(d),
-                )
+
+                def body(rs, k=k):
+                    buf("bs", layer, key)[k, rs, :] = run_sum(layer, key, k, rs).astype(BF)
+
+                row_loop(body, part)
+            cross_copy(layer, key).start()
+
+    def third(layer, key):
+        cs = buf("cs", layer, key)
+        if swaps(layer, key):
+            for cp in run_copies(layer, key):
+                cp.wait_recv()
+
+            def body(rs):
+                cs[rs, :] = run_sum(layer, key, 1 - g, rs).astype(BF)
+
+            row_loop(body, part)
+            last_copy(layer, key).start()
+            return
+
+        @pl.when(s == layer)
+        def _():
+            cross_copy(layer, key).wait_recv()
+            br = buf("br", layer, key)
+
+            def body(rs):
+                cs[rs, :] = (run_sum(layer, key, 1 - g, rs) + br[1 - g, rs, :].astype(F32)).astype(BF)
+
+            row_loop(body, part)
+            last_copy(layer, key).start()
+
+    def fourth(layer, key):
+        cr = buf("cr", layer, key)
+        out, at = out_of(key, layer)
+
+        @pl.when(s == layer)
+        def _():
+            last_copy(layer, key).wait_recv()
+
+            def body(rs):
+                tot = run_sum(layer, key, g, rs) + cr[rs, :].astype(F32)
+                if swaps(layer, key):
+                    out[rs, at : at + tot.shape[1]] = tot
+                else:
+                    out[rs, :] = tot + buf("br", layer, key)[g, rs, :].astype(F32)
+
+            row_loop(body, part)
+
+        if swaps(layer, key):
+
+            @pl.when(s != layer)
+            def _():
+                last_copy(layer, key).wait_recv()
+
+                def body(rs):
+                    tot = run_sum(layer, key, g, rs) + cr[rs, :].astype(F32)
+                    buf("es", layer, key)[rs, :] = tot.astype(BF)
+
+                row_loop(body, part)
+                home_copy(layer, key).start()
+
+    def fifth(layer, key):
+        if swaps(layer, key):
+            out, at = out_of(key, 1 - layer)
+
+            @pl.when(s == layer)
+            def _():
+                home_copy(layer, key).wait_recv()
+
+                def body(rs):
+                    got = buf("er", layer, key)[rs, :].astype(F32)
+                    out[rs, at : at + got.shape[1]] = got
+
+                row_loop(body, part)
+
+    def grads_close():
+        for (layer, key), mode in MODES.items():
+            for cp in run_copies(layer, key):
+                cp.wait_send()
+            if mode == "swap":
+                swap_copy(layer, key).wait_send()
+                last_copy(layer, key).wait_send()
+
+            @pl.when(s == layer)
+            def _(layer=layer, key=key, mode=mode):
+                if mode == "run":
+                    last_copy(layer, key).wait_send()
+
+            @pl.when(s != layer)
+            def _(layer=layer, key=key, mode=mode):
+                (home_copy if mode == "swap" else cross_copy)(layer, key).wait_send()
 
     def rows_of(buf, layer):
         x = buf[layer]
         return x.reshape(full, x.shape[-1])
+
+    stages = (give, second, third, fourth, fifth)
+    spots = {
+        (1, 0): ("1 1du",),
+        (1, 1): ("1 1o", "2 1du"),
+        (1, 2): ("1 1q", "3 1d", "2 1o"),
+        (0, 0): ("1 0d", "3 1u", "2 1q", "3 1o"),
+        (0, 1): ("1 0uo", "4 1d", "2 0d", "3 1q", "4 1uo"),
+        (0, 2): ("1 0q", "3 0d", "5 1d", "2 0u", "5 1o", "4 1q"),
+        (0, 3): ("2 0o", "3 0u", "4 0d", "2 0q", "3 0o", "4 0u", "5 1q", "3 0q"),
+        (0, 4): ("4 0o", "5 0u", "4 0q", "5 0oq"),
+    }
+
+    def serve(layer, spot):
+        for line in spots.get((layer, spot), ()):
+            for key in line[3:]:
+                stages[int(line[0]) - 1](int(line[2]), key)
 
     def back_rows(layer, j, u_buf, r_buf, gain, base, at, extra=None):
         v.stt[...] = jnp.zeros(v.stt.shape, F32)
@@ -567,6 +803,7 @@
         grad_of(layer, "u", rows_of(v.sb, layer), v.du[...].reshape(full, ff))
         ones = jnp.ones((8, full), BF)
         v.smo[layer, 6:7, :] = nn(ones, v.du[...].reshape(full, ff))[0:1]
+        serve(layer, 0)
         sum_end(j)
 
         def at_two(rs, out):
@@ -596,6 +833,7 @@
         v.dgo[layer, :, 0:128] = tile.astype(BF)
         group_send(v.dgo.at[layer], v.dg.at[layer, own_b], v.s_ds.at[layer], v.s_dr.at[layer])
         grad_of(layer, "o", rows_of(v.dhb, layer), rows_of(v.attb, layer))
+        serve(layer, 1)
 
         put_masked(v.ma, v.qa[layer], k_mask)
         put_masked(v.mb, v.dgo[layer], v_mask)
@@ -664,6 +902,7 @@
         grad_of(layer, "q", rows_of(v.nb, layer), v.gm[...].reshape(full, 640))
         v.smo[layer, 7:8, :] = jnp.zeros((1, dim), F32)
         v.smo[layer, 7:8, 0:640] = nn(ones, v.gm[...].reshape(full, 640))[0:1]
+        serve(layer, 2)
         sum_end(j + 1)
 
         def at_one(rs, out):
@@ -682,9 +921,10 @@
     norm_one(0)
     forward(0)
     forward_end(0)
+    red(og, v.gq, 1)
+    forward(1)
     red_wait(og, v.gq, 1)
     send(v.gq.at[0], v.gq.at[1], v.s_xy.at[2], v.s_xy.at[3], me_y)
-    forward(1)
     v.dyf[q_own, :] = v.gq[0].astype(F32)
     remote(v.gq.at[0], v.gq.at[1], v.s_xy.at[2], v.s_xy.at[3], me_y).wait_recv()
     v.dyf[q_oth, :] = v.gq[1].astype(F32)
@@ -698,77 +938,36 @@
     backward_begin(0)
     backward(0)
 
-    for layer in (1, 0):
-        for i in range(4):
-            key = "duoq"[i]
-            for d in range(1, half):
-                for k in range(2):
-                    dst = v.ar.at[layer, d - 1, k, :, pl.ds(col[key], width[key])]
-                    remote(dst, dst, v.s_as.at[layer, i, d, k], v.s_ar.at[layer, i, d, k], zpeer(d)).wait_recv()
-
-    def pair_sum(layer, k, rs):
-        own = pl.ds(pl.multiple_of((zi + half * k) * part + rs.start, 16), RB)
-        tot = v.gr[layer, own, :].astype(F32)
-        for d in range(1, half):
-            tot = tot + v.ar[layer, d - 1, k, rs, :].astype(F32)
-        return tot
-
-    for k in range(2):
-
-        def send_rows(rs, k=k):
-            v.bs[k, rs, :] = pair_sum(1 - s, k, rs).astype(BF)
-
-        row_loop(send_rows, part)
-        send(v.bs.at[k], v.br.at[k], v.s_b.at[0, k], v.s_b.at[1, k], me_x)
-    send(v.smo, v.smc, v.s_sm.at[0], v.s_sm.at[1], me_c).wait_recv()
+    send(v.smo, v.smc, v.s_sm.at[0], v.s_sm.at[1], me_c)
+    remote(v.smo, v.smc, v.s_sm.at[0], v.s_sm.at[1], me_c).wait_recv()
+    rowid = lax.broadcasted_iota(jnp.int32, (8, dim), 0)
     for layer in range(2):
-        rowid = lax.broadcasted_iota(jnp.int32, (8, dim), 0)
         v.smc[layer] = v.smo[layer] + jnp.where(rowid < 6, v.smc[layer], 0.0)
     for k in range(1, 2 * nd):
         other = (s * nd + z + k) % (2 * nd)
         so = other // nd
         send(v.smc.at[so], v.smr.at[k - 1], v.s_sms.at[k - 1], v.s_smr.at[k - 1], (so, other % nd, t))
-
-    def put(rs, tot):
-        for o_ref, key in ((o_d, "d"), (o_u, "u"), (o_o, "o"), (o_q, "q")):
-            o_ref[rs, :] = tot[:, col[key] : col[key] + width[key]]
-
-    for k in (1, 0):
-        kk = (g + k) % 2
-        remote(v.bs.at[kk], v.br.at[kk], v.s_b.at[0, kk], v.s_b.at[1, kk], me_x).wait_recv()
-
-        def add_rows(rs, k=k, kk=kk):
-            tot = pair_sum(s, kk, rs) + v.br[kk, rs, :].astype(F32)
-            if k == 1:
-                v.c2s[rs, :] = tot.astype(BF)
-            else:
-                put(rs, tot)
-
-        row_loop(add_rows, part)
-        if k == 1:
-            send(v.c2s, v.c2r, v.s_c.at[0, 0], v.s_c.at[1, 0], me_o)
+    serve(0, 3)
     for k in range(1, 2 * nd):
         remote(v.smr.at[0], v.smr.at[k - 1], v.s_sms.at[k - 1], v.s_smr.at[k - 1], me_x).wait_recv()
     tot = v.smc[s]
     for k in range(1, 2 * nd):
         tot = tot + v.smr[k - 1]
     o_s[...] = tot
-    remote(v.c2s, v.c2r, v.s_c.at[0, 0], v.s_c.at[1, 0], me_o).wait_recv()
-
-    def last_rows(rs):
-        for o_ref, key in ((o_d, "d"), (o_u, "u"), (o_o, "o"), (o_q, "q")):
-            o_ref[rs, :] += v.c2r[rs, col[key] : col[key] + width[key]].astype(F32)
-
-    row_loop(last_rows, part)
+    serve(0, 4)
 
     for cp in late:
         cp.wait_send()
+
+    grads_close()
     for i, src, dst in ((0, fr, v.xq), (1, og, v.gq)):
 
         @pl.when(keeps)
         def _(i=i, src=src, dst=dst):
             remote(src.at[1 - g], dst.at[0], v.s_red.at[i], v.s_red.at[2 + i], me_o).wait_send()
 
+    for i in range(4):
+        forward_w_end(i)
     put_out_wait(0, 0, acts)
     put_out_wait(1, 1, acts)
     put_out_wait(2, 0, igs)

time: 349 us -> 302 us (0.87)
  the two profiles are of different devices: /device:TPU:24 before, /device:TPU:0 now
where the time goes in v2:
time: 302 us; the launch traced here: 300 us
  Pallas kernels  282 us (93%)
  local copies, waits for them, and re-layouts  12.9 us (4%)
  other arithmetic  4.34 us (1%)
    pallas_call x1, Pallas kernels, local(): pl.pallas_call(functools.partial(mega, nd, (*gathered, *plan) if big else...  282 us

profile of v2, /device:TPU:0, one launch (start us, length us, event | category | flops | bytes accessed | tf_op | source)
XLA Modules:
  0.0 300.0 jit_solution(10722497205913542644)
XLA Ops:
  0.6 0.0 copy-start
  0.7 0.8 slice_reduce_fusion.3
  1.5 0.7 bitcast_convert_fusion.1
  2.2 0.1 pad_convert_fusion
  2.3 0.0 copy-done
  2.3 0.1 reshape.56
  2.4 0.1 eq.17
  2.5 0.7 bitcast_convert_fusion
  3.2 1.9 concatenate.4.refs_6_
  5.2 0.3 broadcast_compare_fusion
  5.4 0.7 select_convert_fusion.1.refs_8_
  6.1 1.0 select_convert_fusion.refs_7_
  7.1 282.0 %shard_map.186 = (bf16[2,88,768]{2,1,0:T(8,128)(2,1)}, bf16[2,88,768]{2,1,0:T(8,128)(2,1)}, f32[192,640]{1,0:T(8,128)}, f32[192,768]{1,0:T(8,128)}, f32[192,256]...) custom-call(bf16[2,88,768]{2,1,0:T(8,128)(2,1)} %refs_0_.1, bf16[2,88,768]{2,1,0:T(8,128)(2,1)} %refs_1_.1, ...), custom_call_target="tpu_custom_call" | custom-call | tf_op jit(solution)/shard_map/pallas_call | solution.py:1017
  289.1 0.0 copy-start.1
  289.1 0.9 slice_reduce_fusion.2
  290.0 0.1 stack.29
  290.1 0.1 stack.30
  290.2 0.1 dynamic-slice_maximum_fusion
  290.3 0.6 copy.27
  290.8 0.8 constant_dynamic-slice_fusion
  291.6 0.8 slice_reduce_fusion
  292.4 0.1 constant_dynamic-slice_fusion.1
  292.5 0.6 broadcast_in_dim.89
  293.0 0.6 slice_bitcast_fusion.5
  293.6 0.6 slice_bitcast_fusion.4
  294.2 1.0 slice_bitcast_fusion
  295.2 0.8 copy.25
  296.0 0.0 copy-done.1
  296.0 0.0 copy-start.5
  296.0 0.0 copy-start.4
  296.0 0.1 slice_bitcast_fusion.3
  296.1 0.0 copy-start.3
  296.1 0.9 maximum_bitcast_fusion
  297.0 0.0 copy-done.5
  297.0 0.0 copy-start.2
  297.0 0.7 copy.32
  297.7 0.0 copy-done.4
  297.7 0.7 copy.33
  298.4 0.0 copy-done.3
  298.4 0.8 copy.34
  299.2 0.0 copy-done.2
  299.2 0.8 copy.35
  (9 shorter events, 0.1 us)
Async XLA Ops:
  0.6 1.6 copy-start
  289.1 6.9 %copy-start.1 = (f32[192,640]{1,0:T(8,128)S(1)}, f32[192,640]{1,0:T(8,128)}, u32[]{:S(2)}) copy-start(f32[192,640]{1,0:T(8,128)} %get-tuple-element.19) | copy-start | bytes 1474564
  296.0 1.0 copy-start.5
  296.0 1.7 copy-start.4
  296.1 2.3 copy-start.3
  297.0 2.2 copy-start.2

commit v3 on v2

--- a/solution.py
+++ b/solution.py
@@ -34,7 +34,8 @@
         "d": (0, ff, ff // 2, ff // 2),
         "u": (ff, ff, ff // 2, ff // 2),
         "o": (2 * ff, 256, 128, 128),
-        "q": (2 * ff + 256, 640, 256, 384),
+        "q": (2 * ff + 256, 256, 128, 128),
+        "k": (2 * ff + 512, 384, 0, 0),
     }[key]
 
 
@@ -42,11 +43,13 @@
     (1, "d"): "swap",
     (1, "u"): "run",
     (1, "o"): "swap",
-    (1, "q"): "swap",
+    (1, "q"): "run",
+    (1, "k"): "run",
     (0, "d"): "run",
     (0, "u"): "swap",
     (0, "o"): "swap",
-    (0, "q"): "swap",
+    (0, "q"): "run",
+    (0, "k"): "run",
 }
 
 
@@ -150,9 +153,9 @@
 
 
 def mega(nd, names, *refs):
-    (fr, og, wq, wo, wu, wd, sp, kf, qf) = refs[:9]
-    (acts, igs, o_q, o_u, o_o, o_d, o_s) = refs[9:16]
-    b_ = dict(zip(names, refs[16:]))
+    (fr, og, wq, wo, wu, wd, gains, moves, bup, bqv, kf) = refs[:11]
+    (acts, igs, o_q, o_u, o_o, o_d, o_s) = refs[11:18]
+    b_ = dict(zip(names, refs[18:]))
     big = nd > MOST
 
     class Bufs:
@@ -203,12 +206,18 @@
         pltpu.make_async_copy(wo, v.wob.at[s, pl.ds(64, 192)], v.s_loc.at[2]),
         pltpu.make_async_copy(wu, v.wub.at[s], v.s_loc.at[3]),
         pltpu.make_async_copy(wd, v.wdb.at[s], v.s_loc.at[4]),
-        pltpu.make_async_copy(sp, v.spb.at[s], v.s_loc.at[5]),
     ]
     for cp in loads:
         cp.start()
     v.wqb[s, pl.ds(192, 64), :] = jnp.zeros((64, dim), BF)
     v.wob[s, pl.ds(0, 64), :] = jnp.zeros((64, dim), BF)
+    hl = bqv.shape[1]
+    v.spb[s, 0:2, :] = gains[...].astype(F32)
+    v.spb[s, 2:6, :] = moves[...].astype(F32)
+    v.spb[s, 6:7, :] = bup[...].astype(F32)
+    v.spb[s, 7:16, :] = jnp.zeros((9, dim), F32)
+    v.spb[s, 7:9, 0:hl] = bqv[...].astype(F32)
+    v.spb[s, 8:16, :] = pltpu.roll(v.spb[s, 8:16, :], hl, 1)
 
     barrier = pltpu.get_barrier_semaphore()
     for k in range(1, 2 * nd):
@@ -238,7 +247,6 @@
     red(fr, v.xq, 0)
     for cp in loads[:2]:
         cp.wait()
-    loads[5].wait()
     mats = (v.wqb, v.wob, v.wub, v.wdb)
 
     def w_parts(i):
@@ -304,7 +312,7 @@
             fn(pl.ds(pl.multiple_of(i * RB, RB), RB))
             return carry
 
-        lax.fori_loop(0, n // RB, step, 0)
+        lax.fori_loop(0, n // RB, step, 0, unroll=n // RB if n == two else 4)
 
     def unit(x):
         cen = x - jnp.mean(x, axis=-1, keepdims=True)
@@ -413,7 +421,9 @@
             rs = pl.ds(pl.multiple_of(hf * two, 16), two)
             q = (r[:, 0:256] + bias_q).astype(BF).astype(F32) * 0.125
             v.qa[layer, rs, 0:128] = q[:, 0:128].astype(BF)
-            v.qa[layer, rs, 128:256] = (q[:, 128:256] + qf[rs, :].astype(F32)).astype(BF)
+            clip = kf[own_b, rs, :].astype(F32) * (1.0 / BIG) + 1.0
+            clip = jnp.where(lane[0:two] >= 80, clip, 0.0)
+            v.qa[layer, rs, 128:256] = (q[:, 128:256] + clip).astype(BF)
             v.kvb[layer, own_b, rs, :] = (r[:, 256:640] + bias_kv).astype(BF)
 
         if layer == 0:
@@ -626,9 +636,9 @@
             tot = tot + buf("ar", layer, key)[d - 1, k, rs, :].astype(F32)
         return tot
 
-    def out_of(key, e=0):
-        _, n, stride, m = shares(key, ff)
-        return dict(d=o_d, u=o_u, o=o_o, q=o_q)[key], e * stride
+    def out_of(layer, key, e):
+        base = e * shares(key, ff)[2] if swaps(layer, key) else 0
+        return dict(d=o_d, u=o_u, o=o_o, q=o_q, k=o_q)[key], base + 256 * (key == "k")
 
     def give(layer, key):
         if swaps(layer, key):
@@ -689,7 +699,7 @@
 
     def fourth(layer, key):
         cr = buf("cr", layer, key)
-        out, at = out_of(key, layer)
+        out, at = out_of(layer, key, layer)
 
         @pl.when(s == layer)
         def _():
@@ -697,10 +707,9 @@
 
             def body(rs):
                 tot = run_sum(layer, key, g, rs) + cr[rs, :].astype(F32)
-                if swaps(layer, key):
-                    out[rs, at : at + tot.shape[1]] = tot
-                else:
-                    out[rs, :] = tot + buf("br", layer, key)[g, rs, :].astype(F32)
+                if not swaps(layer, key):
+                    tot = tot + buf("br", layer, key)[g, rs, :].astype(F32)
+                out[rs, at : at + tot.shape[1]] = tot
 
             row_loop(body, part)
 
@@ -719,7 +728,7 @@
 
     def fifth(layer, key):
         if swaps(layer, key):
-            out, at = out_of(key, 1 - layer)
+            out, at = out_of(layer, key, 1 - layer)
 
             @pl.when(s == layer)
             def _():
@@ -755,13 +764,15 @@
     stages = (give, second, third, fourth, fifth)
     spots = {
         (1, 0): ("1 1du",),
-        (1, 1): ("1 1o", "2 1du"),
-        (1, 2): ("1 1q", "3 1d", "2 1o"),
-        (0, 0): ("1 0d", "3 1u", "2 1q", "3 1o"),
-        (0, 1): ("1 0uo", "4 1d", "2 0d", "3 1q", "4 1uo"),
-        (0, 2): ("1 0q", "3 0d", "5 1d", "2 0u", "5 1o", "4 1q"),
-        (0, 3): ("2 0o", "3 0u", "4 0d", "2 0q", "3 0o", "4 0u", "5 1q", "3 0q"),
-        (0, 4): ("4 0o", "5 0u", "4 0q", "5 0oq"),
+        (1, 1): ("1 1o",),
+        (1, 5): ("2 1du", "1 1q"),
+        (1, 2): ("1 1k", "2 1o"),
+        (0, 0): ("1 0du",),
+        (0, 1): ("1 0o", "2 1qk", "3 1d"),
+        (0, 5): ("1 0q", "2 0du", "3 1o"),
+        (0, 2): ("1 0k", "2 0o", "3 1u", "2 0q"),
+        (0, 3): ("3 0u", "2 0k", "3 0odq", "4 0u", "3 0k", "4 1d", "3 1qk", "4 1uo", "4 0doq", "5 1do"),
+        (0, 4): ("5 0uo", "4 0k", "4 1qk"),
     }
 
     def serve(layer, spot):
@@ -851,6 +862,12 @@
             return carry
 
         lax.fori_loop(0, nd, query_block, 0)
+        for i in range(2):
+            rs = slice(i * two, (i + 1) * two)
+            v.gm[i, :, 0:128] = (v.dqs[rs, 0:128] * 0.125).astype(BF)
+            v.gm[i, :, 128:256] = jnp.where(lane[rs] < 64, v.dqs[rs, 128:256] * 0.125, 0.0).astype(BF)
+        grad_of(layer, "q", rows_of(v.nb, layer), v.gm[:, :, 0:256].reshape(full, 256))
+        serve(layer, 5)
 
         build_kv(layer, own_b)
         put_masked(v.ma, v.kt[...], k_mask)
@@ -893,13 +910,11 @@
 
         for i in range(2):
             rs = slice(i * two, (i + 1) * two)
-            v.gm[i, :, 0:128] = (v.dqs[rs, 0:128] * 0.125).astype(BF)
-            v.gm[i, :, 128:256] = jnp.where(lane[rs] < 64, v.dqs[rs, 128:256] * 0.125, 0.0).astype(BF)
             v.gm[i, :, 256:384] = v.dks[rs, 0:128].astype(BF)
             v.gm[i, :, 384:512] = jnp.where(lane[rs] < 64, v.dks[rs, 128:256], v.dvs[rs, 0:128]).astype(BF)
             v.gm[i, :, 512:640] = v.dvs[rs, 128:256].astype(BF)
         sum_begin(j + 1, lambda hf: nn(v.gm[hf], v.wqb[layer]))
-        grad_of(layer, "q", rows_of(v.nb, layer), v.gm[...].reshape(full, 640))
+        grad_of(layer, "k", rows_of(v.nb, layer), v.gm[:, :, 256:640].reshape(full, 384))
         v.smo[layer, 7:8, :] = jnp.zeros((1, dim), F32)
         v.smo[layer, 7:8, 0:640] = nn(ones, v.gm[...].reshape(full, 640))[0:1]
         serve(layer, 2)
@@ -974,6 +989,32 @@
     put_out_wait(3, 1, igs)
 
 
+def lay_out(nd, a_in, i_in, q_in, u_in, o_in, d_in, sums, acts, igs, g_q, bias, g_o, g_u, upb, g_d, gain, shift, sq):
+    for src, dst in ((a_in, acts), (i_in, igs), (u_in, g_u), (d_in, g_d)):
+        dst[...] = src[...]
+    z, t = lax.axis_index("dp"), lax.axis_index("tensor")
+    part, dim = u_in.shape[0], sums.shape[1]
+    hl = g_q.shape[2]
+    heads, _, hw = bias.shape
+    g_q[0] = q_in[:, 0:hl]
+    g_q[1] = q_in[:, 256 : 256 + hl]
+    g_q[2] = pltpu.roll(q_in[:, 384:640], 192, 1)[:, 0:hl]
+    sq[0:part, :] = o_in[...]
+    g_o[...] = sq[...].T[64 : 64 + hl, 0:part]
+
+    def from_lane(lo, n):
+        return pltpu.roll(sums[...], (dim - lo) % dim, 1)[:, 0:n]
+
+    for h in range(heads):
+        bias[h, 0:1, :] = from_lane(h * HD + z * hw, hw)[7:8]
+        bias[h, 1:2, :] = from_lane(256 + hl + h * HD + z * hw, hw)[7:8]
+        uw = upb.shape[2]
+        upb[h] = from_lane((h * nd + z) * uw, uw)[6:7]
+    norms = from_lane((z * 4 + t) * gain.shape[1], gain.shape[1])
+    gain[...] = norms[0:2]
+    shift[...] = norms[2:6]
+
+
 def local(frames, out_grad, clip_ids, w_qkv, bias_qv, w_out, w_up, bias_up, w_down, ln_gain, shifts):
     rows, dim = frames.shape[1:]
     nd = lax.axis_size("dp")
@@ -983,17 +1024,6 @@
     ff = w_up.shape[2]
     part = dim // nd
     wide = w_qkv[0].transpose(1, 2, 0).reshape(3 * hl, dim)
-    zeros = functools.partial(jnp.zeros, dtype=F32)
-    params = jnp.concatenate(
-        [
-            ln_gain[0].astype(F32),
-            shifts[0].astype(F32),
-            bias_up.astype(F32),
-            jnp.pad(bias_qv[0, 0].astype(F32), (0, dim - hl))[None],
-            jnp.pad(bias_qv[0, 1].astype(F32), (hl, dim - 2 * hl))[None],
-            zeros((7, dim)),
-        ]
-    )
     clip = lax.dynamic_index_in_dim(clip_ids, z // half, 0, keepdims=False)
     clip = clip.reshape(nd, 4, rows)
     clip = jnp.stack([clip[:, 0], clip[:, 2], clip[:, 1], clip[:, 3]], axis=1).reshape(nd, 4 * rows)
@@ -1003,9 +1033,6 @@
     k_feat = jnp.where(
         (lane >= 64) & (lane < 73), 1.0, jnp.where(spot & jnp.logical_not(same), -BIG, 0.0)
     ).astype(BF)
-    own_b = z % half + half * s
-    q_feat = jnp.where(spot & lax.dynamic_index_in_dim(same, own_b, 0, keepdims=False), 1.0, 0.0).astype(BF)
-
     plan = scratch_plan(nd, rows, dim, hl, ff)
     shape = jax.ShapeDtypeStruct
     anyspec = pl.BlockSpec(memory_space=pl.ANY)
@@ -1026,34 +1053,45 @@
             shape((8, dim), F32),
         )
         + tuple(shape(dims, BF) for dims in gathered.values()) * big,
-        in_specs=[anyspec] * 7 + [vspec] * 2,
+        in_specs=[anyspec] * 6 + [vspec] * 5,
         out_specs=(anyspec,) * 2 + (vspec,) * 5 + (anyspec,) * (2 * big),
         scratch_shapes=list(plan.values()),
         compiler_params=pltpu.CompilerParams(
             collective_id=0, has_side_effects=True, vmem_limit_bytes=63 * 1024 * 1024
         ),
-    )(frames, out_grad, wide, w_out[0], w_up[0], w_down[0], params, k_feat, q_feat)
-
-    acts, igs, g_q, g_u, g_o, g_d, small = outs[:7]
-    g_qkv = jnp.stack([g_q[:, 0:hl], g_q[:, 256 : 256 + hl], g_q[:, 256 + hl : 256 + 2 * hl]], axis=1)
-    bias = small[7]
-    bias = jnp.stack([bias[0:hl], bias[256 + hl : 256 + 2 * hl]]).reshape(2, hl // HD, HD)
-    bias = lax.dynamic_slice_in_dim(bias, z * (HD // nd), HD // nd, 2)
-    upb = small[6].reshape(hl // HD, ff // (hl // HD))
-    upb = lax.dynamic_slice_in_dim(upb, z * (upb.shape[1] // nd), upb.shape[1] // nd, 1)
-    own = dim // (4 * nd)
-    norms = lax.dynamic_slice_in_dim(small, (z * 4 + t) * own, own, 1)
+    )(frames, out_grad, wide, w_out[0], w_up[0], w_down[0], ln_gain[0], shifts[0], bias_up, bias_qv[0], k_feat)
+
+    own, hw, uw = dim // (4 * nd), HD // nd, ff // (hl // HD) // nd
+    heads = hl // HD
+    acts, igs, g_q, bias, g_o, g_u, upb, g_d, gain, shift = pl.pallas_call(
+        functools.partial(lay_out, nd),
+        out_shape=(
+            shape((2, rows, dim), BF),
+            shape((2, rows, dim), BF),
+            shape((3, part, hl), F32),
+            shape((heads, 2, hw), F32),
+            shape((hl, part), F32),
+            shape((part, ff), F32),
+            shape((heads, 1, uw), F32),
+            shape((part, ff), F32),
+            shape((2, own), F32),
+            shape((4, own), F32),
+        ),
+        in_specs=[vspec] * 7,
+        out_specs=(vspec,) * 10,
+        scratch_shapes=[pltpu.VMEM((256, 256), F32)],
+    )(*outs[:7])
     return (
         acts[None],
         igs[None],
-        g_qkv[None],
-        bias[None],
-        g_o[:, 64 : 64 + hl].T[None],
+        g_q.transpose(1, 0, 2)[None],
+        bias.transpose(1, 0, 2)[None],
+        g_o[None],
         g_u[None],
-        upb[None],
+        upb.transpose(1, 0, 2),
         g_d.T[None],
-        norms[None, 0:2],
-        norms[None, 2:6],
+        gain[None],
+        shift[None],
     )
 
 

time: 302 us -> 275 us (0.911)
  Pallas kernels: 282 us -> 268 us
  local copies, waits for them, and re-layouts: 12.9 us -> 0.87 us
  other arithmetic: 4.34 us -> 1.02 us
    pallas_call x1, Pallas kernels: 282 us -> 265 us  [local(): pl.pallas_call(functools.partial(mega, nd, (*gathered, *plan) if big else...]
    pallas_call x0 -> x1, Pallas kernels: none -> 3.28 us  [local(): pl.pallas_call(functools.partial(lay_out, nd), out_shape=(shape((2, rows,...]
    unnamed x17 -> x2, local copies, waits for them, and re-layouts: 3.87 us -> 0.66 us
where the time goes in v3:
time: 275 us; the launch traced here: 271 us
  Pallas kernels  268 us (97%)
    pallas_call x1, Pallas kernels, local(): pl.pallas_call(functools.partial(mega, nd, (*gathered, *plan) if big else...  265 us

profile of v3, /device:TPU:0, one launch (start us, length us, event | category | flops | bytes accessed | tf_op | source)
XLA Modules:
  0.0 271.3 jit_solution(5440468570367343902)
XLA Ops:
  0.6 0.0 copy-start
  0.7 0.7 copy-done
  1.4 0.1 reshape.37
  1.5 0.1 eq.15
  1.6 1.0 select_convert_fusion.refs_10_
  2.6 265.1 %shard_map.186 = (bf16[2,88,768]{2,1,0:T(8,128)(2,1)}, bf16[2,88,768]{2,1,0:T(8,128)(2,1)}, f32[192,640]{1,0:T(8,128)}, f32[192,768]{1,0:T(8,128)}, f32[192,256]...) custom-call(bf16[2,88,768]{2,1,0:T(8,128)(2,1)} %refs_0_.1, bf16[2,88,768]{2,1,0:T(8,128)(2,1)} %refs_1_.1, ...), custom_call_target="tpu_custom_call" | custom-call | tf_op jit(solution)/shard_map/pallas_call | solution.py:1044
  267.7 3.3 %shard_map.187 = (bf16[2,88,768]{2,1,0:T(8,128)(2,1)}, bf16[2,88,768]{2,1,0:T(8,128)(2,1)}, f32[3,192,192]{2,1,0:T(8,128)}, f32[3,2,16]{2,1,0:T(2,128)}, f32[192...) custom-call(bf16[2,88,768]{2,1,0:T(8,128)(2,1)} %get-tuple-element.2, ...), custom_call_target="tpu_custom_call" | custom-call | tf_op jit(solution)/shard_map/pallas_call | solution.py:1066
  (5 shorter events, 0.1 us)
Async XLA Ops:
  0.6 0.7 copy-start

commit v4 on v3

--- a/solution.py
+++ b/solution.py
@@ -113,9 +113,9 @@
         s_loc=dma((12,)),
         s_red=dma((4,)),
         s_xy=dma((4,)),
-        s_wx=dma((2, 9)),
-        s_wzs=dma((8, half)),
-        s_wzr=dma((8, half)),
+        s_wx=dma((2, 13)),
+        s_wzs=dma((12, half)),
+        s_wzr=dma((12, half)),
         s_ag=dma((2, 8)),
         s_cc=dma((2, SLOTS)),
         s_yy=dma((2, SLOTS)),
@@ -250,7 +250,11 @@
     mats = (v.wqb, v.wob, v.wub, v.wdb)
 
     def w_parts(i):
-        return 2 if mats[i].shape[1] // half % 32 == 0 else 1
+        n = (2, 2, 2, 3)[i]
+        return n if mats[i].shape[1] // half % (16 * n) == 0 else 1
+
+    def straight(i, e):
+        return i == 3 and e == 2
 
     def w_rows(i, p, e):
         n = mats[i].shape[1] // half
@@ -260,9 +264,13 @@
     def ship(i):
         for e in range(w_parts(i)):
             src = mats[i].at[s, w_rows(i, zi, e)]
-            send(src, src, v.s_wx.at[0, 2 * i + e], v.s_wx.at[1, 2 * i + e], me_x)
-
-    send(v.spb.at[s], v.spb.at[s], v.s_wx.at[0, 8], v.s_wx.at[1, 8], me_x)
+            send(src, src, v.s_wx.at[0, 3 * i + e], v.s_wx.at[1, 3 * i + e], me_x)
+        for e in range(w_parts(i)):
+            for d in range(1, half) if straight(i, e) else ():
+                src = mats[i].at[s, w_rows(i, (zi + half - d) % half, e)]
+                remote(src, src, v.s_wzs.at[3 * i + e, d], v.s_wzr.at[3 * i + e, d], me_x).start()
+
+    send(v.spb.at[s], v.spb.at[s], v.s_wx.at[0, 12], v.s_wx.at[1, 12], me_x)
     ship(0)
     loads[2].wait()
     ship(1)
@@ -272,14 +280,14 @@
 
     def w_copy(i, e, d, back=0):
         src = mats[i].at[1 - s, w_rows(i, (zi + back) % half, e)]
-        return remote(src, src, v.s_wzs.at[2 * i + e, d], v.s_wzr.at[2 * i + e, d], zpeer(d))
+        return remote(src, src, v.s_wzs.at[3 * i + e, d], v.s_wzr.at[3 * i + e, d], zpeer(d))
 
     def forward_w(i, e=None):
         for e in range(w_parts(i)) if e is None else (e,):
             if e < w_parts(i):
                 src = mats[i].at[1 - s, w_rows(i, zi, e)]
-                remote(src, src, v.s_wx.at[0, 2 * i + e], v.s_wx.at[1, 2 * i + e], me_x).wait_recv()
-                for d in range(1, half):
+                remote(src, src, v.s_wx.at[0, 3 * i + e], v.s_wx.at[1, 3 * i + e], me_x).wait_recv()
+                for d in () if straight(i, e) else range(1, half):
                     w_copy(i, e, d).start()
 
     def forward_w_end(i):
@@ -296,7 +304,7 @@
 
     red_wait(fr, v.xq, 0)
     send(v.xq.at[0], v.xq.at[1], v.s_xy.at[0], v.s_xy.at[1], me_y)
-    remote(v.spb.at[s], v.spb.at[s], v.s_wx.at[0, 8], v.s_wx.at[1, 8], me_x).wait_recv()
+    remote(v.spb.at[s], v.spb.at[s], v.s_wx.at[0, 12], v.s_wx.at[1, 12], me_x).wait_recv()
     q_own = pl.ds(pl.multiple_of(rows * y, 8), rows)
     q_oth = pl.ds(pl.multiple_of(rows * (1 - y), 8), rows)
     v.xres[q_own, :] = v.xq[0].astype(F32)
@@ -429,6 +437,8 @@
         if layer == 0:
             forward_w(0, 1)
         gather_w(0, layer)
+        if layer == 0:
+            forward_w(1)
         qkv(c)
         share_wait(v.nb, layer, layer)
         qkv(1 - c)
@@ -449,11 +459,10 @@
                 remote(dst, dst, v.s_kvs.at[layer, 0], v.s_kvr.at[layer, bk], me_x).wait_recv()
 
             if layer == 0:
-                for i in (1, 2):
-
-                    @pl.when(k == i)
-                    def _(i=i):
-                        forward_w(i)
+
+                @pl.when(k == 1)
+                def _():
+                    forward_w(2)
 
             build_kv(layer, bk)
             kt, vt = v.kt[...], v.vt[...]
@@ -508,6 +517,7 @@
         share(v.sb, layer, 2 + layer)
         if layer == 0:
             forward_w(3, 1)
+            forward_w(3, 2)
         gather_w(2, layer)
         bias_up = prow(layer, 6)
 
@@ -770,8 +780,8 @@
         (0, 0): ("1 0du",),
         (0, 1): ("1 0o", "2 1qk", "3 1d"),
         (0, 5): ("1 0q", "2 0du", "3 1o"),
-        (0, 2): ("1 0k", "2 0o", "3 1u", "2 0q"),
-        (0, 3): ("3 0u", "2 0k", "3 0odq", "4 0u", "3 0k", "4 1d", "3 1qk", "4 1uo", "4 0doq", "5 1do"),
+        (0, 2): ("1 0k", "2 0o", "2 0q"),
+        (0, 3): ("3 0u", "2 0k", "3 0odq", "4 0u", "3 0k", "3 1u", "4 1d", "3 1qk", "4 1uo", "4 0doq", "5 1do"),
         (0, 4): ("5 0uo", "4 0k", "4 1qk"),
     }
 

time: 275 us -> 269 us (0.978)
  Pallas kernels: 268 us -> 263 us
    pallas_call x1, Pallas kernels: 265 us -> 260 us  [local(): pl.pallas_call(functools.partial(mega, nd, (*gathered, *plan) if big else...]
where the time goes in v4:
time: 269 us; the launch traced here: 266 us
  Pallas kernels  263 us (98%)
    pallas_call x1, Pallas kernels, local(): pl.pallas_call(functools.partial(mega, nd, (*gathered, *plan) if big else...  260 us

profile of v4, /device:TPU:0, one launch (start us, length us, event | category | flops | bytes accessed | tf_op | source)
XLA Modules:
  0.0 266.1 jit_solution(13430172662740483455)
XLA Ops:
  0.6 0.0 copy-start
  0.7 0.7 copy-done
  1.4 0.1 reshape.37
  1.5 0.1 eq.15
  1.6 1.0 select_convert_fusion.refs_10_
  2.6 259.9 %shard_map.186 = (bf16[2,88,768]{2,1,0:T(8,128)(2,1)}, bf16[2,88,768]{2,1,0:T(8,128)(2,1)}, f32[192,640]{1,0:T(8,128)}, f32[192,768]{1,0:T(8,128)}, f32[192,256]...) custom-call(bf16[2,88,768]{2,1,0:T(8,128)(2,1)} %refs_0_.1, bf16[2,88,768]{2,1,0:T(8,128)(2,1)} %refs_1_.1, ...), custom_call_target="tpu_custom_call" | custom-call | tf_op jit(solution)/shard_map/pallas_call | solution.py:1054
  262.5 3.3 %shard_map.187 = (bf16[2,88,768]{2,1,0:T(8,128)(2,1)}, bf16[2,88,768]{2,1,0:T(8,128)(2,1)}, f32[3,192,192]{2,1,0:T(8,128)}, f32[3,2,16]{2,1,0:T(2,128)}, f32[192...) custom-call(bf16[2,88,768]{2,1,0:T(8,128)(2,1)} %get-tuple-element.2, ...), custom_call_target="tpu_custom_call" | custom-call | tf_op jit(solution)/shard_map/pallas_call | solution.py:1076
  (5 shorter events, 0.1 us)
Async XLA Ops:
  0.6 0.7 copy-start

commit v5 on v4

--- a/solution.py
+++ b/solution.py
@@ -118,9 +118,9 @@
         s_wzr=dma((12, half)),
         s_ag=dma((2, 8)),
         s_cc=dma((2, SLOTS)),
-        s_yy=dma((2, SLOTS)),
-        s_kvs=dma((2, nd)),
-        s_kvr=dma((2, nd)),
+        s_yy=dma((2, SLOTS, 2)),
+        s_kvs=dma((2, nd, 2)),
+        s_kvr=dma((2, nd, 2)),
         s_qs=dma((2, nd)),
         s_qr=dma((2, nd)),
         s_ds=dma((2, nd)),
@@ -315,12 +315,13 @@
     def prow(layer, i):
         return v.spb[layer, i : i + 1, :]
 
-    def row_loop(fn, n=two):
+    def row_loop(fn, n=two, first=0):
         def step(i, carry):
             fn(pl.ds(pl.multiple_of(i * RB, RB), RB))
             return carry
 
-        lax.fori_loop(0, n // RB, step, 0, unroll=n // RB if n == two else 4)
+        count = n // RB - first // RB
+        lax.fori_loop(first // RB, n // RB, step, 0, unroll=count if n <= two else 4)
 
     def unit(x):
         cen = x - jnp.mean(x, axis=-1, keepdims=True)
@@ -360,12 +361,22 @@
             v.chip[j % 2, rs, :] = tot
             v.ys[j % 2, rs, :] = tot.astype(BF)
 
-        row_loop(body)
-        remote(v.ys.at[j % 2], v.yr.at[k], v.s_yy.at[0, k], v.s_yy.at[1, k], me_y).start()
-
-    def sum_end(j):
-        k = j % SLOTS
-        remote(v.ys.at[j % 2], v.yr.at[k], v.s_yy.at[0, k], v.s_yy.at[1, k], me_y).wait()
+        for e in range(2):
+            row_loop(body, cuts[e + 1], cuts[e])
+            chip_copy(j, e).start()
+
+    cuts = (0, (two // RB + 1) // 2 * RB, two)
+
+    def chip_copy(j, e):
+        k, rs = j % SLOTS, pl.ds(cuts[e], cuts[e + 1] - cuts[e])
+        return remote(
+            v.ys.at[j % 2, rs], v.yr.at[k, rs], v.s_yy.at[0, k, e], v.s_yy.at[1, k, e], me_y
+        )
+
+    def sum_end(j, body):
+        for e in range(2):
+            chip_copy(j, e).wait()
+            row_loop(body, cuts[e + 1], cuts[e])
 
     def sum_rows(j, rs):
         k = j % SLOTS
@@ -439,10 +450,16 @@
         gather_w(0, layer)
         if layer == 0:
             forward_w(1)
+        def kv_send(hf):
+            src = v.kvb.at[layer, own_b, pl.ds(pl.multiple_of(hf * two, 16), two)]
+            for k in range(1, nd):
+                send(src, src, v.s_kvs.at[layer, k, hf], v.s_kvr.at[layer, own_b, hf], member(k)[0])
+
         qkv(c)
+        kv_send(c)
         share_wait(v.nb, layer, layer)
         qkv(1 - c)
-        group_send(v.kvb.at[layer, own_b], v.kvb.at[layer, own_b], v.s_kvs.at[layer], v.s_kvr.at[layer])
+        kv_send(1 - c)
 
         put_masked(v.ma, v.qa[layer], k_mask)
         v.mst[...] = jnp.full(v.mst.shape, -3e38, F32)
@@ -455,8 +472,9 @@
 
             @pl.when(k > 0)
             def _():
-                dst = v.kvb.at[layer, bk]
-                remote(dst, dst, v.s_kvs.at[layer, 0], v.s_kvr.at[layer, bk], me_x).wait_recv()
+                for e in range(2):
+                    dst = v.kvb.at[layer, bk, pl.ds(e * two, two)]
+                    remote(dst, dst, v.s_kvs.at[layer, 0, e], v.s_kvr.at[layer, bk, e], me_x).wait_recv()
 
             if layer == 0:
 
@@ -502,7 +520,6 @@
                 group_send(v.qa.at[one], v.qg.at[one, own_b], v.s_qs.at[one], v.s_qr.at[one])
         if layer == 0:
             forward_w(3, 0)
-        sum_end(2 * layer)
         out_bias, gain2, shift2 = prow(layer, 4), prow(layer, 1), prow(layer, 3)
 
         def body(rs):
@@ -513,7 +530,7 @@
             v.r2[layer, rs, :] = r
             v.sb[layer, c, rs, :] = (u * gain2 + shift2).astype(BF)
 
-        row_loop(body)
+        sum_end(2 * layer, body)
         share(v.sb, layer, 2 + layer)
         if layer == 0:
             forward_w(3, 1)
@@ -539,14 +556,13 @@
         sum_begin(2 * layer + 1, lambda hf: nn(v.gl[layer, hf], v.wdb[layer]))
 
     def forward_end(layer):
-        sum_end(2 * layer + 1)
         out_bias = prow(layer, 5)
 
         def body(rs):
             out = v.hid[rs, :] + sum_rows(2 * layer + 1, rs) + out_bias
             v.xres[rs, :] = out.astype(BF).astype(F32)
 
-        row_loop(body)
+        sum_end(2 * layer + 1, body)
         if layer == 0:
             norm_one(1)
         put_out(layer, layer, v.xres, acts)
@@ -808,7 +824,7 @@
             v.stt[2] += out
             v.stt[3] += inn
 
-        row_loop(body)
+        sum_end(j, body)
 
     def backward_begin(layer):
         def d_second(hf):
@@ -825,7 +841,6 @@
         ones = jnp.ones((8, full), BF)
         v.smo[layer, 6:7, :] = nn(ones, v.du[...].reshape(full, ff))[0:1]
         serve(layer, 0)
-        sum_end(j)
 
         def at_two(rs, out):
             v.dhf[rs, :] = out
@@ -928,7 +943,6 @@
         v.smo[layer, 7:8, :] = jnp.zeros((1, dim), F32)
         v.smo[layer, 7:8, 0:640] = nn(ones, v.gm[...].reshape(full, 640))[0:1]
         serve(layer, 2)
-        sum_end(j + 1)
 
         def at_one(rs, out):
             low = out.astype(BF)

time: 269 us -> 269 us (level)
  no operation moved by 1% of the time
where the time goes in v5:
time: 269 us; the launch traced here: 266 us
  Pallas kernels  263 us (98%)
    pallas_call x1, Pallas kernels, local(): pl.pallas_call(functools.partial(mega, nd, (*gathered, *plan) if big else...  260 us

profile of v5, /device:TPU:0, one launch (start us, length us, event | category | flops | bytes accessed | tf_op | source)
XLA Modules:
  0.0 266.1 jit_solution(8649818013079347717)
XLA Ops:
  0.6 0.0 copy-start
  0.7 0.7 copy-done
  1.4 0.1 reshape.37
  1.5 0.1 eq.15
  1.6 1.0 select_convert_fusion.refs_10_
  2.6 259.9 %shard_map.186 = (bf16[2,88,768]{2,1,0:T(8,128)(2,1)}, bf16[2,88,768]{2,1,0:T(8,128)(2,1)}, f32[192,640]{1,0:T(8,128)}, f32[192,768]{1,0:T(8,128)}, f32[192,256]...) custom-call(bf16[2,88,768]{2,1,0:T(8,128)(2,1)} %refs_0_.1, bf16[2,88,768]{2,1,0:T(8,128)(2,1)} %refs_1_.1, ...), custom_call_target="tpu_custom_call" | custom-call | tf_op jit(solution)/shard_map/pallas_call | solution.py:1068
  262.5 3.3 %shard_map.187 = (bf16[2,88,768]{2,1,0:T(8,128)(2,1)}, bf16[2,88,768]{2,1,0:T(8,128)(2,1)}, f32[3,192,192]{2,1,0:T(8,128)}, f32[3,2,16]{2,1,0:T(2,128)}, f32[192...) custom-call(bf16[2,88,768]{2,1,0:T(8,128)(2,1)} %get-tuple-element.2, ...), custom_call_target="tpu_custom_call" | custom-call | tf_op jit(solution)/shard_map/pallas_call | solution.py:1090
  (5 shorter events, 0.1 us)
Async XLA Ops:
  0.6 0.7 copy-start

commit v6 on v5

--- a/solution.py
+++ b/solution.py
@@ -421,7 +421,7 @@
         return hi, mid, (x - hi) - mid
 
     def group_send(src, dst, ss, rs):
-        for k in range(1, nd):
+        for k in range(nd - 1, 0, -1):
             dev, _ = member(k)
             send(src, dst, ss.at[k], rs.at[own_b], dev)
 
@@ -452,7 +452,7 @@
             forward_w(1)
         def kv_send(hf):
             src = v.kvb.at[layer, own_b, pl.ds(pl.multiple_of(hf * two, 16), two)]
-            for k in range(1, nd):
+            for k in range(nd - 1, 0, -1):
                 send(src, src, v.s_kvs.at[layer, k, hf], v.s_kvr.at[layer, own_b, hf], member(k)[0])
 
         qkv(c)

time: 269 us -> 271 us (level)
  no operation moved by 1% of the time
where the time goes in v6:
time: 271 us; the launch traced here: 267 us
  Pallas kernels  264 us (97%)
    pallas_call x1, Pallas kernels, local(): pl.pallas_call(functools.partial(mega, nd, (*gathered, *plan) if big else...  261 us

profile of v6, /device:TPU:0, one launch (start us, length us, event | category | flops | bytes accessed | tf_op | source)
XLA Modules:
  0.0 267.2 jit_solution(7980792507563771354)
XLA Ops:
  0.6 0.0 copy-start
  0.7 0.7 copy-done
  1.4 0.1 reshape.37
  1.5 0.1 eq.15
  1.6 1.0 select_convert_fusion.refs_10_
  2.6 261.0 %shard_map.186 = (bf16[2,88,768]{2,1,0:T(8,128)(2,1)}, bf16[2,88,768]{2,1,0:T(8,128)(2,1)}, f32[192,640]{1,0:T(8,128)}, f32[192,768]{1,0:T(8,128)}, f32[192,256]...) custom-call(bf16[2,88,768]{2,1,0:T(8,128)(2,1)} %refs_0_.1, bf16[2,88,768]{2,1,0:T(8,128)(2,1)} %refs_1_.1, ...), custom_call_target="tpu_custom_call" | custom-call | tf_op jit(solution)/shard_map/pallas_call | solution.py:1068
  263.6 3.3 %shard_map.187 = (bf16[2,88,768]{2,1,0:T(8,128)(2,1)}, bf16[2,88,768]{2,1,0:T(8,128)(2,1)}, f32[3,192,192]{2,1,0:T(8,128)}, f32[3,2,16]{2,1,0:T(2,128)}, f32[192...) custom-call(bf16[2,88,768]{2,1,0:T(8,128)(2,1)} %get-tuple-element.2, ...), custom_call_target="tpu_custom_call" | custom-call | tf_op jit(solution)/shard_map/pallas_call | solution.py:1090
  (5 shorter events, 0.1 us)
Async XLA Ops:
  0.6 0.7 copy-start
